TPU v7x, 32 devices: a whole 2x2x4 slice. The times are simulated.
32 devices in a mesh: farm: 2 (over x), body: 16 (over z, y, core).
Axes of the slice: x: 2, y: 2, z: 4, core: 2. Of those that a mesh axis runs over, the one named last changes fastest.
Arguments:
- incident: float32 [32, 2, 16, 768], P(('farm', 'body')), parts along dimension 0, may hold values from -6 to 6
- self_inverse: float32 [32, 2, 768, 768], P(('farm', 'body')), parts along dimension 0
- cross_blocks: float32 [32, 4, 2, 768, 768], P(('farm', 'body')), parts along dimension 0, may hold values from -0.046875 to 0.046875
- neighbours: int32 [32, 4], P(('farm', 'body')), parts along dimension 0, may hold values from -1 to 15, as said below
- panel_weight: float32 [32, 768], P(('farm', 'body')), parts along dimension 0, may hold values from -0.0546875 to 0.0546875
Outputs:
- sources: float32 [32, 2, 16, 768], P(('farm', 'body')), parts along dimension 0
- farm_force: float32 [2, 2, 16], P('farm'), parts along dimension 0
There are 2 independent parts, one for each index of `farm`. A program takes and returns all parts, laid end to end along the dimension named above; each array names one. Nothing has to cross between parts.
Inputs may be any that keep to these rules, and one draw needn't show every extreme that they name: `neighbours`: each row names distinct bodies other than its own, each within 8 positions of it around the closed loop of 16 bodies; some body names the body exactly 8 positions away.
All inputs are finite; a program needn't handle non-finite values.
Results may differ from a plain program's by a relative error of at most 0.0003.
Values sent between devices are 32-bit elements; how exact they have to be, the bound alone decides.
No kernel may reach another device: no remote copies, remote signals or barrier semaphores. Data moves between devices by JAX's collectives and lax.ppermute only.
A program may use at most 128 MiB of HBM per device.

v0:
```python
import functools

import jax
import jax.numpy as jnp
from jax import lax
from jax.experimental import pallas as pl
from jax.experimental.pallas import tpu as pltpu
from jax.sharding import PartitionSpec as P

ITERS = 6
NT = (((1,), (1,)), ((), ()))
LIMIT = 14 * 2**20
VMEM = pl.BlockSpec(memory_space=pltpu.VMEM)
SMEM = pl.BlockSpec(memory_space=pltpu.SMEM)
HBM = pl.BlockSpec(memory_space=pltpu.HBM)


def split(x):
    hi = x.astype(jnp.bfloat16)
    lo = (x - hi.astype(jnp.float32)).astype(jnp.bfloat16)
    return hi, lo


def turn(x, heads):
    return jnp.concatenate([-x[heads:], x[:heads]], axis=0)


def split_all(src, wide, buffers, sems, base=0):
    _, rows, cols = src.shape
    count = 2 * wide.shape[1] // cols
    depth, chunk, _ = buffers.shape
    steps = [(j, r) for j in range(count) for r in range(0, rows, chunk)]

    def copy(i):
        j, r = steps[i]
        return pltpu.make_async_copy(
            src.at[base + j, pl.ds(r, chunk)], buffers.at[i % depth], sems.at[i % depth]
        )

    for i in range(min(depth, len(steps))):
        copy(i).start()
    for i, (j, r) in enumerate(steps):
        copy(i).wait()
        hi, lo = split(buffers[i % depth])
        slot, c = j // 2, j % 2
        at = 2 * c * rows + r
        wide[at:at + chunk, slot * cols:(slot + 1) * cols] = hi
        wide[at + rows:at + rows + chunk, slot * cols:(slot + 1) * cols] = lo
        if i + depth < len(steps):
            copy(i + depth).start()


def put_field(lhs, slot, x):
    rows, panels = x.shape
    hi, lo = split(x)
    lhs[:rows, slot * panels:(slot + 1) * panels] = hi
    lhs[rows:, slot * panels:(slot + 1) * panels] = lo


def product(lhs, wides, heads):
    panels = wides[0].shape[0] // 4
    rows = 2 * heads

    def real(c):
        total = None
        for part in range(2):
            row, at = (2 * c + part) * panels, 0
            for wide in wides:
                width = wide.shape[1]
                term = lax.dot_general(
                    wide[row:row + panels, :], lhs[:, at:at + width], NT,
                    preferred_element_type=jnp.float32,
                )
                total = term if total is None else total + term
                at += width
        flat = total.T
        return flat[:rows] + flat[rows:]

    return real(0) + turn(real(1), heads)


def first_kernel(heads, inverse, field_ref, wide, out_ref, lhs, buffers, sems):
    split_all(inverse, wide, buffers, sems)
    put_field(lhs, 0, field_ref[...])
    out_ref[...] = product(lhs, [wide], heads)


def near_kernel(src, field_ref, wide, same_ref, buffers, sems):
    split_all(src, wide, buffers, sems)
    same_ref[...] = field_ref[...]


def late_kernel(base, src, waited, wide, buffers, sems):
    del waited
    split_all(src, wide, buffers, sems, base)


def after_kernel(*refs):
    del refs


def after(a, b, *others):
    here = pl.BlockSpec(memory_space=pl.ANY)
    like = jax.ShapeDtypeStruct(a.shape, a.dtype)
    return pl.pallas_call(
        after_kernel,
        in_specs=[here] * (2 + len(others)),
        out_specs=[here] * 2,
        out_shape=[like] * 2,
        input_output_aliases={0: 0, 1: 1},
        compiler_params=pltpu.CompilerParams(vmem_limit_bytes=2**20),
    )(a, b, *others)


def sweep_kernel(heads, slots, places, last, row_ref, *refs):
    count = len(places)
    blocks = dict(zip(places, refs[:count]))
    field_ref, cross_a, cross_b, inverse = refs[count:count + 4]
    refs = refs[count + 4:]
    if last:
        weight_ref, out_ref, part_ref, near, lhs, short = refs
    else:
        out_ref, near, lhs, short = refs
    me = lax.axis_index("body")
    lines = count // 4
    for k in range(slots):
        index = row_ref[0, k]
        dz = lax.rem(me // 4 + lines - index // 4, lines)
        at = dz * 4 + jnp.bitwise_xor(lax.rem(index, 4), lax.rem(me, 4))
        at = jnp.where(index < 0, -1, at)
        for j in range(count):
            @pl.when(at == j)
            def _():
                near[...] = blocks[j][...]

        @pl.when(index < 0)
        def _():
            near[...] = jnp.zeros_like(near)

        put_field(lhs, k, near[...])

    put_field(short, 0, field_ref[...] - product(lhs, [cross_a, cross_b], heads))
    value = product(short, [inverse], heads)
    out_ref[...] = value
    if last:
        for c in range(2):
            part_ref[c:c + 1, :] = lax.dot_general(
                weight_ref[...], value[c * heads:(c + 1) * heads], NT,
                precision=lax.Precision.HIGHEST, preferred_element_type=jnp.float32,
            )


def body(count, incident, self_inverse, cross_blocks, neighbours, panel_weight):
    _, _, heads, panels = incident.shape
    slots = cross_blocks.shape[1]
    rows = 2 * heads
    field = incident.reshape(rows, panels)
    lines = count // 4
    out = jax.ShapeDtypeStruct((rows, panels), jnp.float32)
    tiny = jax.ShapeDtypeStruct((2, heads), jnp.float32)
    params = pltpu.CompilerParams(vmem_limit_bytes=LIMIT)
    chunk = panels // 2
    inverse, sources = pl.pallas_call(
        functools.partial(first_kernel, heads),
        in_specs=[HBM, VMEM],
        out_specs=[VMEM, VMEM],
        out_shape=[jax.ShapeDtypeStruct((4 * panels, panels), jnp.bfloat16), out],
        scratch_shapes=[
            pltpu.VMEM((2 * rows, panels), jnp.bfloat16),
            pltpu.VMEM((4, chunk, panels), jnp.float32),
            pltpu.SemaphoreType.DMA((4,)),
        ],
        compiler_params=params,
    )(pltpu.with_memory_space_constraint(self_inverse[0], pltpu.HBM), field)
    early = slots // 2
    all_blocks = pltpu.with_memory_space_constraint(
        cross_blocks[0].reshape(2 * slots, panels, panels), pltpu.HBM
    )
    scratch = [pltpu.VMEM((6, chunk, panels), jnp.float32), pltpu.SemaphoreType.DMA((6,))]

    def cost(count):
        size = count * 8 * panels * panels
        return pl.CostEstimate(flops=4 * size, bytes_accessed=size, transcendentals=0)

    cross_a, same = pl.pallas_call(
        near_kernel,
        in_specs=[HBM, VMEM],
        out_specs=[VMEM, VMEM],
        out_shape=[jax.ShapeDtypeStruct((4 * panels, early * panels), jnp.bfloat16), out],
        scratch_shapes=scratch,
        compiler_params=params,
        cost_estimate=cost(early),
    )(all_blocks, sources)
    split_late = pl.pallas_call(
        functools.partial(late_kernel, 2 * early),
        in_specs=[HBM, pl.BlockSpec(memory_space=pl.ANY)],
        out_specs=VMEM,
        out_shape=jax.ShapeDtypeStruct((4 * panels, (slots - early) * panels), jnp.bfloat16),
        scratch_shapes=scratch,
        compiler_params=params,
        cost_estimate=cost(slots - early),
    )

    def sweep(last, *args):
        return pl.pallas_call(
            functools.partial(sweep_kernel, heads, slots, places, last),
            in_specs=[SMEM] + [VMEM] * (len(args) - 1),
            out_specs=[VMEM, VMEM] if last else VMEM,
            out_shape=[out, tiny] if last else out,
            scratch_shapes=[
                pltpu.VMEM((rows, panels), jnp.float32),
                pltpu.VMEM((2 * rows, slots * panels), jnp.bfloat16),
                pltpu.VMEM((2 * rows, panels), jnp.bfloat16),
            ],
            compiler_params=params,
        )(*args)

    def move(x, pairs):
        return lax.ppermute(x, "body", pairs)

    z_pairs = [[(i, (i + 4 * d) % count) for i in range(count)] for d in range(lines)]
    y_pairs = [(i, i ^ 2) for i in range(count)]
    c_pairs = [(i, i ^ 1) for i in range(count)]
    order = sorted(range(1, lines), key=lambda d: min(d, lines - d))
    places = [4 * d + j for d in order[::-1] + [0] for j in range(4)]
    for step in range(ITERS):
        blocks = [None] * count
        own = sources if step else same
        blocks[0] = sources
        for d in order:
            blocks[4 * d] = move(own if d == order[-1] else sources, z_pairs[d])
        far = order[-1]
        blocks[2] = move(sources, y_pairs)
        if not step:
            cross_b = split_late(all_blocks, same)
            ends = [4 * order[0], 4 * order[-2]]
            blocks[ends[0]], blocks[ends[1]] = after(*[blocks[e] for e in ends], cross_b)
        blocks[4 * far + 2] = move(own, [(i, j ^ 2) for i, j in z_pairs[far]])
        for d in order[:-1]:
            blocks[4 * d + 2] = move(blocks[4 * d], y_pairs)
        passed = [blocks[4 * d + 2] for d in order[:-1]]
        pair = after(blocks[4 * far], blocks[4 * far + 2], *passed)
        blocks[4 * far], blocks[4 * far + 2] = pair
        for d in [0] + order:
            blocks[4 * d + 1] = move(blocks[4 * d], c_pairs)
            blocks[4 * d + 3] = move(blocks[4 * d + 2], c_pairs)
        args = (neighbours, *[blocks[j] for j in places], field, cross_a, cross_b, inverse)
        if step == ITERS - 1:
            sources, part = sweep(True, *args, panel_weight)
        else:
            sources = sweep(False, *args)
    terms = [part] + [move(part, z_pairs[d]) for d in range(1, lines)]
    while len(terms) > 1:
        half = len(terms) // 2
        terms = [terms[i] + terms[i + half] for i in range(half)]
    part = terms[0]
    part = part + move(part, y_pairs)
    part = part + move(part, c_pairs)
    return (sources.reshape(1, 2, heads, panels), part[None])


def solution(mesh):
    return jax.shard_map(
        functools.partial(body, mesh.shape["body"]),
        mesh=mesh,
        in_specs=(
            P(("farm", "body"), None, None, None),
            P(("farm", "body"), None, None, None),
            P(("farm", "body"), None, None, None, None),
            P(("farm", "body"), None),
            P(("farm", "body"), None),
        ),
        out_specs=(P(("farm", "body"), None, None, None), P("farm", None, None)),
        check_vma=False,
    )
```

profile of v0, /device:TPU:0, one launch (start us, length us, event | category | flops | bytes accessed | tf_op | source)
XLA Modules:
  0.0 188.0 jit_solution(13797857480544340635)
XLA Ops:
  1.5 3.9 %shard_map.68 = (bf16[3072,768]{1,0:T(8,128)(2,1)S(1)}, f32[32,768]{1,0:T(8,128)S(1)}) custom-call(f32[2,768,768]{2,1,0:T(8,128)} %bitcast.15, f32[32,768]{1,0:T(8,128)S(1)} %bitcast.6), custom_call_target="tpu_custom_call" | custom-call | tf_op jit(solution)/shard_map/pallas_call | solution.py:163
  5.4 3.0 %collective-permute-start.13 = (f32[32,768]{1,0:T(8,128)S(1)}, f32[32,768]{1,0:T(8,128)S(1)}, u32[]{:S(2)}, u32[]{:S(2)}) collective-permute-start(f32[32,768]{1,0:T(8,128)S(1)} %get-tuple-element.22.field_ref.refs_12_), channel_id=1, source_target_pairs={{0,2},{1,3},{2,0},{3,1},{4,6},{5,7},{6,4},{7,5},{8,10},{9,11},{10,... | collective-permute-start | bytes 294920 | tf_op jit(solution)/shard_map/ppermute | solution.py:219
  8.4 3.6 %collective-permute-start.3 = (f32[32,768]{1,0:T(8,128)S(1)}, f32[32,768]{1,0:T(8,128)S(1)}, u32[]{:S(2)}, u32[]{:S(2)}) collective-permute-start(f32[32,768]{1,0:T(8,128)S(1)} %get-tuple-element.22.field_ref.refs_12_), channel_id=1, source_target_pairs={{0,12},{1,13},{2,14},{3,15},{4,0},{5,1},{6,2},{7,3},{8,4},{9,5},{1... | collective-permute-start | bytes 294920 | tf_op jit(solution)/shard_map/ppermute | solution.py:219
  12.0 4.1 %shard_map.69 = (bf16[3072,1536]{1,0:T(8,128)(2,1)S(1)}, f32[32,768]{1,0:T(8,128)S(1)}) custom-call(f32[8,768,768]{2,1,0:T(8,128)} %bitcast.13, f32[32,768]{1,0:T(8,128)S(1)} %get-tuple-element.22.field_ref.refs_12_), custom_call_target="tpu_custom_call" | custom-call | flops 37748736 | bytes 9437184 | tf_op jit(solution)/shard_map/pallas_call | solution.py:185
  17.2 1.9 %collective-permute-start = (f32[32,768]{1,0:T(8,128)S(1)}, f32[32,768]{1,0:T(8,128)S(1)}, u32[]{:S(2)}, u32[]{:S(2)}) collective-permute-start(f32[32,768]{1,0:T(8,128)S(1)} %get-tuple-element.23.waited), channel_id=1, source_target_pairs={{0,8},{1,9},{2,10},{3,11},{4,12},{5,13},{6,14},{7,15},{8,0},{9,1},... | collective-permute-start | bytes 294920 | tf_op jit(solution)/shard_map/ppermute | solution.py:219
  19.1 4.1 %shard_map.70.refs_2_.refs_18_ = bf16[3072,1536]{1,0:T(8,128)(2,1)S(1)} custom-call(f32[8,768,768]{2,1,0:T(8,128)} %bitcast.14, f32[32,768]{1,0:T(8,128)S(1)} %get-tuple-element.23.waited), custom_call_target="tpu_custom_call" | custom-call | flops 37748736 | bytes 9437184 | tf_op jit(solution)/shard_map/pallas_call | solution.py:235
  23.3 1.6 collective-permute-start.4
  25.4 1.5 collective-permute-done.1.refs_1_
  28.4 1.1 collective-permute-done.5.refs_3_.refs_6_
  31.5 7.3 %shard_map.73.refs_12_ = f32[32,768]{1,0:T(8,128)S(1)} custom-call(s32[1,4]{1,0:T(1,128)S(1)} %copy-done.2, f32[32,768]{1,0:T(8,128)S(1)} %get-tuple-element.26.refs_0_, f32[32,768]{1,0:T(8,128)S(1)} %collective-permute-done.6.refs_1_, f32[32,768]{1,0:T(8,128)S(1)} %get-tuple-element.27.refs_2_, f32[32,768]{1,0:T(8,128)S(1)} %collective-permute-done.7.refs_3_, ...), custom_call_target="tpu_custom_call" | custom-call | tf_op jit(solution)/shard_map/pallas_call | solution.py:205
  38.9 3.9 %collective-permute-start.19 = (f32[32,768]{1,0:T(8,128)S(1)}, f32[32,768]{1,0:T(8,128)S(1)}, u32[]{:S(2)}, u32[]{:S(2)}) collective-permute-start(f32[32,768]{1,0:T(8,128)S(1)} %shard_map.73.refs_12_), channel_id=1, source_target_pairs={{0,12},{1,13},{2,14},{3,15},{4,0},{5,1},{6,2},{7,3},{8,4},{9,5},{1... | collective-permute-start | bytes 294920 | tf_op jit(solution)/shard_map/ppermute | solution.py:219
  44.8 2.3 %collective-permute-start.15 = (f32[32,768]{1,0:T(8,128)S(1)}, f32[32,768]{1,0:T(8,128)S(1)}, u32[]{:S(2)}, u32[]{:S(2)}) collective-permute-start(f32[32,768]{1,0:T(8,128)S(1)} %shard_map.73.refs_12_), channel_id=1, source_target_pairs={{0,8},{1,9},{2,10},{3,11},{4,12},{5,13},{6,14},{7,15},{8,0},{9,1},... | collective-permute-start | bytes 294920 | tf_op jit(solution)/shard_map/ppermute | solution.py:219
  48.2 2.1 %collective-permute-done.17.refs_8_ = f32[32,768]{1,0:T(8,128)S(1)} collective-permute-done((f32[32,768]{1,0:T(8,128)S(1)}, f32[32,768]{1,0:T(8,128)S(1)}, u32[]{:S(2)}, u32[]{:S(2)}) %collective-permute-start.17) | collective-permute-done | bytes 98336 | tf_op jit(solution)/shard_map/ppermute | solution.py:219
  51.4 4.9 %collective-permute-done.16.refs_1_ = f32[32,768]{1,0:T(8,128)S(1)} collective-permute-done((f32[32,768]{1,0:T(8,128)S(1)}, f32[32,768]{1,0:T(8,128)S(1)}, u32[]{:S(2)}, u32[]{:S(2)}) %collective-permute-start.16) | collective-permute-done | bytes 98336 | tf_op jit(solution)/shard_map/ppermute | solution.py:219
  56.3 1.5 collective-permute-done.15.refs_0_
  60.4 7.5 %shard_map.75.refs_12_ = f32[32,768]{1,0:T(8,128)S(1)} custom-call(s32[1,4]{1,0:T(1,128)S(1)} %copy-done.2, f32[32,768]{1,0:T(8,128)S(1)} %get-tuple-element.30.refs_0_, f32[32,768]{1,0:T(8,128)S(1)} %collective-permute-done.21.refs_1_, f32[32,768]{1,0:T(8,128)S(1)} %get-tuple-element.31.refs_2_, f32[32,768]{1,0:T(8,128)S(1)} %collective-permute-done.22.refs_3_, ...), custom_call_target="tpu_custom_call" | custom-call | tf_op jit(solution)/shard_map/pallas_call | solution.py:205
  67.9 1.7 collective-permute-start.34
  71.8 2.6 %collective-permute-start.30 = (f32[32,768]{1,0:T(8,128)S(1)}, f32[32,768]{1,0:T(8,128)S(1)}, u32[]{:S(2)}, u32[]{:S(2)}) collective-permute-start(f32[32,768]{1,0:T(8,128)S(1)} %shard_map.75.refs_12_), channel_id=1, source_target_pairs={{0,8},{1,9},{2,10},{3,11},{4,12},{5,13},{6,14},{7,15},{8,0},{9,1},... | collective-permute-start | bytes 294920 | tf_op jit(solution)/shard_map/ppermute | solution.py:219
  75.5 1.8 collective-permute-done.32.refs_8_
  78.3 4.8 %collective-permute-done.31.refs_1_ = f32[32,768]{1,0:T(8,128)S(1)} collective-permute-done((f32[32,768]{1,0:T(8,128)S(1)}, f32[32,768]{1,0:T(8,128)S(1)}, u32[]{:S(2)}, u32[]{:S(2)}) %collective-permute-start.31) | collective-permute-done | bytes 98336 | tf_op jit(solution)/shard_map/ppermute | solution.py:219
  83.1 1.5 collective-permute-done.30.refs_0_
  87.2 7.4 %shard_map.77.refs_12_ = f32[32,768]{1,0:T(8,128)S(1)} custom-call(s32[1,4]{1,0:T(1,128)S(1)} %copy-done.2, f32[32,768]{1,0:T(8,128)S(1)} %get-tuple-element.32.refs_0_, f32[32,768]{1,0:T(8,128)S(1)} %collective-permute-done.36.refs_1_, f32[32,768]{1,0:T(8,128)S(1)} %get-tuple-element.33.refs_2_, f32[32,768]{1,0:T(8,128)S(1)} %collective-permute-done.37.refs_3_, ...), custom_call_target="tpu_custom_call" | custom-call | tf_op jit(solution)/shard_map/pallas_call | solution.py:205
  94.6 1.7 collective-permute-start.49
  98.4 2.7 %collective-permute-start.45 = (f32[32,768]{1,0:T(8,128)S(1)}, f32[32,768]{1,0:T(8,128)S(1)}, u32[]{:S(2)}, u32[]{:S(2)}) collective-permute-start(f32[32,768]{1,0:T(8,128)S(1)} %shard_map.77.refs_12_), channel_id=1, source_target_pairs={{0,8},{1,9},{2,10},{3,11},{4,12},{5,13},{6,14},{7,15},{8,0},{9,1},... | collective-permute-start | bytes 294920 | tf_op jit(solution)/shard_map/ppermute | solution.py:219
  101.0 1.1 collective-permute-start.50
  102.1 1.7 collective-permute-done.47.refs_8_
  103.8 1.1 collective-permute-start.48
  104.9 4.8 %collective-permute-done.46.refs_1_ = f32[32,768]{1,0:T(8,128)S(1)} collective-permute-done((f32[32,768]{1,0:T(8,128)S(1)}, f32[32,768]{1,0:T(8,128)S(1)}, u32[]{:S(2)}, u32[]{:S(2)}) %collective-permute-start.46) | collective-permute-done | bytes 98336 | tf_op jit(solution)/shard_map/ppermute | solution.py:219
  109.7 1.5 collective-permute-done.45.refs_0_
  113.8 7.6 %shard_map.79.refs_12_ = f32[32,768]{1,0:T(8,128)S(1)} custom-call(s32[1,4]{1,0:T(1,128)S(1)} %copy-done.2, f32[32,768]{1,0:T(8,128)S(1)} %get-tuple-element.34.refs_0_, f32[32,768]{1,0:T(8,128)S(1)} %collective-permute-done.51.refs_1_, f32[32,768]{1,0:T(8,128)S(1)} %get-tuple-element.35.refs_2_, f32[32,768]{1,0:T(8,128)S(1)} %collective-permute-done.52.refs_3_, ...), custom_call_target="tpu_custom_call" | custom-call | tf_op jit(solution)/shard_map/pallas_call | solution.py:205
  121.4 1.7 collective-permute-start.64
  125.2 2.6 %collective-permute-start.60 = (f32[32,768]{1,0:T(8,128)S(1)}, f32[32,768]{1,0:T(8,128)S(1)}, u32[]{:S(2)}, u32[]{:S(2)}) collective-permute-start(f32[32,768]{1,0:T(8,128)S(1)} %shard_map.79.refs_12_), channel_id=1, source_target_pairs={{0,8},{1,9},{2,10},{3,11},{4,12},{5,13},{6,14},{7,15},{8,0},{9,1},... | collective-permute-start | bytes 294920 | tf_op jit(solution)/shard_map/ppermute | solution.py:219
  128.9 1.8 collective-permute-done.62.refs_8_
  131.7 4.8 %collective-permute-done.61.refs_1_ = f32[32,768]{1,0:T(8,128)S(1)} collective-permute-done((f32[32,768]{1,0:T(8,128)S(1)}, f32[32,768]{1,0:T(8,128)S(1)}, u32[]{:S(2)}, u32[]{:S(2)}) %collective-permute-start.61) | collective-permute-done | bytes 98336 | tf_op jit(solution)/shard_map/ppermute | solution.py:219
  136.6 1.5 collective-permute-done.60.refs_0_
  140.7 7.3 %shard_map.81.refs_12_ = f32[32,768]{1,0:T(8,128)S(1)} custom-call(s32[1,4]{1,0:T(1,128)S(1)} %copy-done.2, f32[32,768]{1,0:T(8,128)S(1)} %get-tuple-element.36.refs_0_, f32[32,768]{1,0:T(8,128)S(1)} %collective-permute-done.66.refs_1_, f32[32,768]{1,0:T(8,128)S(1)} %get-tuple-element.37.refs_2_, f32[32,768]{1,0:T(8,128)S(1)} %collective-permute-done.67.refs_3_, ...), custom_call_target="tpu_custom_call" | custom-call | tf_op jit(solution)/shard_map/pallas_call | solution.py:205
  148.1 1.7 collective-permute-start.79
  151.9 2.6 %collective-permute-start.75 = (f32[32,768]{1,0:T(8,128)S(1)}, f32[32,768]{1,0:T(8,128)S(1)}, u32[]{:S(2)}, u32[]{:S(2)}) collective-permute-start(f32[32,768]{1,0:T(8,128)S(1)} %shard_map.81.refs_12_), channel_id=1, source_target_pairs={{0,8},{1,9},{2,10},{3,11},{4,12},{5,13},{6,14},{7,15},{8,0},{9,1},... | collective-permute-start | bytes 294920 | tf_op jit(solution)/shard_map/ppermute | solution.py:219
  155.6 1.8 collective-permute-done.77.refs_8_
  158.4 4.8 %collective-permute-done.76.refs_1_ = f32[32,768]{1,0:T(8,128)S(1)} collective-permute-done((f32[32,768]{1,0:T(8,128)S(1)}, f32[32,768]{1,0:T(8,128)S(1)}, u32[]{:S(2)}, u32[]{:S(2)}) %collective-permute-start.76) | collective-permute-done | bytes 98336 | tf_op jit(solution)/shard_map/ppermute | solution.py:219
  163.2 1.5 collective-permute-done.75.refs_0_
  167.3 8.3 %shard_map.83 = (f32[32,768]{1,0:T(8,128)}, f32[2,16]{1,0:T(2,128)S(1)}) custom-call(s32[1,4]{1,0:T(1,128)S(1)} %copy-done.2, f32[32,768]{1,0:T(8,128)S(1)} %get-tuple-element.38.refs_0_, f32[32,768]{1,0:T(8,128)S(1)} %collective-permute-done.81.refs_1_, f32[32,768]{1,0:T(8,128)S(1)} %get-tuple-element.39.refs_2_, ...), custom_call_target="tpu_custom_call" | custom-call | tf_op jit(solution)/shard_map/pallas_call | solution.py:205
  175.6 1.7 collective-permute-start.92
  177.9 1.3 collective-permute-done.92
  179.2 3.5 %collective-permute-done.91 = f32[2,16]{1,0:T(2,128)S(1)} collective-permute-done((f32[2,16]{1,0:T(2,128)S(1)}, f32[2,16]{1,0:T(2,128)S(1)}, u32[]{:S(2)}, u32[]{:S(2)}) %collective-permute-start.91) | collective-permute-done | bytes 160 | tf_op jit(solution)/shard_map/ppermute | solution.py:219
  182.7 1.1 collective-permute-start.93
  183.8 2.6 %collective-permute-done.93 = f32[2,16]{1,0:T(2,128)S(1)} collective-permute-done((f32[2,16]{1,0:T(2,128)S(1)}, f32[2,16]{1,0:T(2,128)S(1)}, u32[]{:S(2)}, u32[]{:S(2)}) %collective-permute-start.93) | collective-permute-done | bytes 160 | tf_op jit(solution)/shard_map/ppermute | solution.py:219
  186.3 1.1 collective-permute-done.94
  (169 shorter events, 38.9 us)
Async XLA Ops:
  5.4 20.0 %collective-permute-start.13 = (f32[32,768]{1,0:T(8,128)S(1)}, f32[32,768]{1,0:T(8,128)S(1)}, u32[]{:S(2)}, u32[]{:S(2)}) collective-permute-start(f32[32,768]{1,0:T(8,128)S(1)} %get-tuple-element.22.field_ref.refs_12_), channel_id=1, source_target_pairs={{0,2},{1,3},{2,0},{3,1},{4,6},{5,7},{6,4},{7,5},{8,10},{9,11},{10,... | collective-permute-start | bytes 294920 | tf_op jit(solution)/shard_map/ppermute | solution.py:219
  8.4 14.9 %collective-permute-start.3 = (f32[32,768]{1,0:T(8,128)S(1)}, f32[32,768]{1,0:T(8,128)S(1)}, u32[]{:S(2)}, u32[]{:S(2)}) collective-permute-start(f32[32,768]{1,0:T(8,128)S(1)} %get-tuple-element.22.field_ref.refs_12_), channel_id=1, source_target_pairs={{0,12},{1,13},{2,14},{3,15},{4,0},{5,1},{6,2},{7,3},{8,4},{9,5},{1... | collective-permute-start | bytes 294920 | tf_op jit(solution)/shard_map/ppermute | solution.py:219
  12.0 11.3 %collective-permute-start.2 = (f32[32,768]{1,0:T(8,128)S(1)}, f32[32,768]{1,0:T(8,128)S(1)}, u32[]{:S(2)}, u32[]{:S(2)}) collective-permute-start(f32[32,768]{1,0:T(8,128)S(1)} %get-tuple-element.22.field_ref.refs_12_), channel_id=1, source_target_pairs={{0,4},{1,5},{2,6},{3,7},{4,8},{5,9},{6,10},{7,11},{8,12},{9,13},{1... | collective-permute-start | bytes 294920 | tf_op jit(solution)/shard_map/ppermute | solution.py:219
  16.2 10.7 %collective-permute-start.1 = (f32[32,768]{1,0:T(8,128)S(1)}, f32[32,768]{1,0:T(8,128)S(1)}, u32[]{:S(2)}, u32[]{:S(2)}) collective-permute-start(f32[32,768]{1,0:T(8,128)S(1)} %get-tuple-element.23.waited), channel_id=1, source_target_pairs={{0,10},{1,11},{2,8},{3,9},{4,14},{5,15},{6,12},{7,13},{8,2},{9,3},... | collective-permute-start | bytes 294920 | tf_op jit(solution)/shard_map/ppermute | solution.py:219
  17.2 10.2 %collective-permute-start = (f32[32,768]{1,0:T(8,128)S(1)}, f32[32,768]{1,0:T(8,128)S(1)}, u32[]{:S(2)}, u32[]{:S(2)}) collective-permute-start(f32[32,768]{1,0:T(8,128)S(1)} %get-tuple-element.23.waited), channel_id=1, source_target_pairs={{0,8},{1,9},{2,10},{3,11},{4,12},{5,13},{6,14},{7,15},{8,0},{9,1},... | collective-permute-start | bytes 294920 | tf_op jit(solution)/shard_map/ppermute | solution.py:219
  23.3 5.1 %collective-permute-start.4 = (f32[32,768]{1,0:T(8,128)S(1)}, f32[32,768]{1,0:T(8,128)S(1)}, u32[]{:S(2)}, u32[]{:S(2)}) collective-permute-start(f32[32,768]{1,0:T(8,128)S(1)} %get-tuple-element.24.refs_8_), channel_id=1, source_target_pairs={{0,2},{1,3},{2,0},{3,1},{4,6},{5,7},{6,4},{7,5},{8,10},{9,11},{10,... | collective-permute-start | bytes 294920 | tf_op jit(solution)/shard_map/ppermute | solution.py:219
  38.9 8.3 %collective-permute-start.19 = (f32[32,768]{1,0:T(8,128)S(1)}, f32[32,768]{1,0:T(8,128)S(1)}, u32[]{:S(2)}, u32[]{:S(2)}) collective-permute-start(f32[32,768]{1,0:T(8,128)S(1)} %shard_map.73.refs_12_), channel_id=1, source_target_pairs={{0,12},{1,13},{2,14},{3,15},{4,0},{5,1},{6,2},{7,3},{8,4},{9,5},{1... | collective-permute-start | bytes 294920 | tf_op jit(solution)/shard_map/ppermute | solution.py:219
  42.7 7.5 %collective-permute-start.17 = (f32[32,768]{1,0:T(8,128)S(1)}, f32[32,768]{1,0:T(8,128)S(1)}, u32[]{:S(2)}, u32[]{:S(2)}) collective-permute-start(f32[32,768]{1,0:T(8,128)S(1)} %shard_map.73.refs_12_), channel_id=1, source_target_pairs={{0,4},{1,5},{2,6},{3,7},{4,8},{5,9},{6,10},{7,11},{8,12},{9,13},{1... | collective-permute-start | bytes 294920 | tf_op jit(solution)/shard_map/ppermute | solution.py:219
  42.7 8.6 %collective-permute-start.28 = (f32[32,768]{1,0:T(8,128)S(1)}, f32[32,768]{1,0:T(8,128)S(1)}, u32[]{:S(2)}, u32[]{:S(2)}) collective-permute-start(f32[32,768]{1,0:T(8,128)S(1)} %shard_map.73.refs_12_), channel_id=1, source_target_pairs={{0,2},{1,3},{2,0},{3,1},{4,6},{5,7},{6,4},{7,5},{8,10},{9,11},{10,... | collective-permute-start | bytes 294920 | tf_op jit(solution)/shard_map/ppermute | solution.py:219
  43.8 12.5 %collective-permute-start.16 = (f32[32,768]{1,0:T(8,128)S(1)}, f32[32,768]{1,0:T(8,128)S(1)}, u32[]{:S(2)}, u32[]{:S(2)}) collective-permute-start(f32[32,768]{1,0:T(8,128)S(1)} %shard_map.73.refs_12_), channel_id=1, source_target_pairs={{0,10},{1,11},{2,8},{3,9},{4,14},{5,15},{6,12},{7,13},{8,2},{9,3},... | collective-permute-start | bytes 294920 | tf_op jit(solution)/shard_map/ppermute | solution.py:219
  44.8 12.9 %collective-permute-start.15 = (f32[32,768]{1,0:T(8,128)S(1)}, f32[32,768]{1,0:T(8,128)S(1)}, u32[]{:S(2)}, u32[]{:S(2)}) collective-permute-start(f32[32,768]{1,0:T(8,128)S(1)} %shard_map.73.refs_12_), channel_id=1, source_target_pairs={{0,8},{1,9},{2,10},{3,11},{4,12},{5,13},{6,14},{7,15},{8,0},{9,1},... | collective-permute-start | bytes 294920 | tf_op jit(solution)/shard_map/ppermute | solution.py:219
  47.1 10.7 %collective-permute-start.20 = (f32[32,768]{1,0:T(8,128)S(1)}, f32[32,768]{1,0:T(8,128)S(1)}, u32[]{:S(2)}, u32[]{:S(2)}) collective-permute-start(f32[32,768]{1,0:T(8,128)S(1)} %collective-permute-done.19.refs_4_), channel_id=1, source_target_pairs={{0,2},{1,3},{2,0},{3,1},{4,6},{5,7},{6,4},{7,5},{8,10},{9,11},{10,... | collective-permute-start | bytes 294920 | tf_op jit(solution)/shard_map/ppermute | solution.py:219
  50.3 8.0 %collective-permute-start.18 = (f32[32,768]{1,0:T(8,128)S(1)}, f32[32,768]{1,0:T(8,128)S(1)}, u32[]{:S(2)}, u32[]{:S(2)}) collective-permute-start(f32[32,768]{1,0:T(8,128)S(1)} %collective-permute-done.17.refs_8_), channel_id=1, source_target_pairs={{0,2},{1,3},{2,0},{3,1},{4,6},{5,7},{6,4},{7,5},{8,10},{9,11},{10,... | collective-permute-start | bytes 294920 | tf_op jit(solution)/shard_map/ppermute | solution.py:219
  51.4 7.0 %collective-permute-start.27 = (f32[32,768]{1,0:T(8,128)S(1)}, f32[32,768]{1,0:T(8,128)S(1)}, u32[]{:S(2)}, u32[]{:S(2)}) collective-permute-start(f32[32,768]{1,0:T(8,128)S(1)} %shard_map.73.refs_12_), channel_id=1, source_target_pairs={{0,1},{1,0},{2,3},{3,2},{4,5},{5,4},{6,7},{7,6},{8,9},{9,8},{10,11... | collective-permute-start | bytes 294920 | tf_op jit(solution)/shard_map/ppermute | solution.py:219
  67.9 6.5 %collective-permute-start.34 = (f32[32,768]{1,0:T(8,128)S(1)}, f32[32,768]{1,0:T(8,128)S(1)}, u32[]{:S(2)}, u32[]{:S(2)}) collective-permute-start(f32[32,768]{1,0:T(8,128)S(1)} %shard_map.75.refs_12_), channel_id=1, source_target_pairs={{0,12},{1,13},{2,14},{3,15},{4,0},{5,1},{6,2},{7,3},{8,4},{9,5},{1... | collective-permute-start | bytes 294920 | tf_op jit(solution)/shard_map/ppermute | solution.py:219
  69.7 7.6 %collective-permute-start.32 = (f32[32,768]{1,0:T(8,128)S(1)}, f32[32,768]{1,0:T(8,128)S(1)}, u32[]{:S(2)}, u32[]{:S(2)}) collective-permute-start(f32[32,768]{1,0:T(8,128)S(1)} %shard_map.75.refs_12_), channel_id=1, source_target_pairs={{0,4},{1,5},{2,6},{3,7},{4,8},{5,9},{6,10},{7,11},{8,12},{9,13},{1... | collective-permute-start | bytes 294920 | tf_op jit(solution)/shard_map/ppermute | solution.py:219
  70.0 8.3 %collective-permute-start.43 = (f32[32,768]{1,0:T(8,128)S(1)}, f32[32,768]{1,0:T(8,128)S(1)}, u32[]{:S(2)}, u32[]{:S(2)}) collective-permute-start(f32[32,768]{1,0:T(8,128)S(1)} %shard_map.75.refs_12_), channel_id=1, source_target_pairs={{0,2},{1,3},{2,0},{3,1},{4,6},{5,7},{6,4},{7,5},{8,10},{9,11},{10,... | collective-permute-start | bytes 294920 | tf_op jit(solution)/shard_map/ppermute | solution.py:219
  71.1 12.0 %collective-permute-start.31 = (f32[32,768]{1,0:T(8,128)S(1)}, f32[32,768]{1,0:T(8,128)S(1)}, u32[]{:S(2)}, u32[]{:S(2)}) collective-permute-start(f32[32,768]{1,0:T(8,128)S(1)} %shard_map.75.refs_12_), channel_id=1, source_target_pairs={{0,10},{1,11},{2,8},{3,9},{4,14},{5,15},{6,12},{7,13},{8,2},{9,3},... | collective-permute-start | bytes 294920 | tf_op jit(solution)/shard_map/ppermute | solution.py:219
  71.8 12.8 %collective-permute-start.30 = (f32[32,768]{1,0:T(8,128)S(1)}, f32[32,768]{1,0:T(8,128)S(1)}, u32[]{:S(2)}, u32[]{:S(2)}) collective-permute-start(f32[32,768]{1,0:T(8,128)S(1)} %shard_map.75.refs_12_), channel_id=1, source_target_pairs={{0,8},{1,9},{2,10},{3,11},{4,12},{5,13},{6,14},{7,15},{8,0},{9,1},... | collective-permute-start | bytes 294920 | tf_op jit(solution)/shard_map/ppermute | solution.py:219
  74.4 10.2 %collective-permute-start.35 = (f32[32,768]{1,0:T(8,128)S(1)}, f32[32,768]{1,0:T(8,128)S(1)}, u32[]{:S(2)}, u32[]{:S(2)}) collective-permute-start(f32[32,768]{1,0:T(8,128)S(1)} %collective-permute-done.34.refs_4_), channel_id=1, source_target_pairs={{0,2},{1,3},{2,0},{3,1},{4,6},{5,7},{6,4},{7,5},{8,10},{9,11},{10,... | collective-permute-start | bytes 294920 | tf_op jit(solution)/shard_map/ppermute | solution.py:219
  77.2 7.9 %collective-permute-start.33 = (f32[32,768]{1,0:T(8,128)S(1)}, f32[32,768]{1,0:T(8,128)S(1)}, u32[]{:S(2)}, u32[]{:S(2)}) collective-permute-start(f32[32,768]{1,0:T(8,128)S(1)} %collective-permute-done.32.refs_8_), channel_id=1, source_target_pairs={{0,2},{1,3},{2,0},{3,1},{4,6},{5,7},{6,4},{7,5},{8,10},{9,11},{10,... | collective-permute-start | bytes 294920 | tf_op jit(solution)/shard_map/ppermute | solution.py:219
  78.3 6.9 %collective-permute-start.42 = (f32[32,768]{1,0:T(8,128)S(1)}, f32[32,768]{1,0:T(8,128)S(1)}, u32[]{:S(2)}, u32[]{:S(2)}) collective-permute-start(f32[32,768]{1,0:T(8,128)S(1)} %shard_map.75.refs_12_), channel_id=1, source_target_pairs={{0,1},{1,0},{2,3},{3,2},{4,5},{5,4},{6,7},{7,6},{8,9},{9,8},{10,11... | collective-permute-start | bytes 294920 | tf_op jit(solution)/shard_map/ppermute | solution.py:219
  94.6 6.5 %collective-permute-start.49 = (f32[32,768]{1,0:T(8,128)S(1)}, f32[32,768]{1,0:T(8,128)S(1)}, u32[]{:S(2)}, u32[]{:S(2)}) collective-permute-start(f32[32,768]{1,0:T(8,128)S(1)} %shard_map.77.refs_12_), channel_id=1, source_target_pairs={{0,12},{1,13},{2,14},{3,15},{4,0},{5,1},{6,2},{7,3},{8,4},{9,5},{1... | collective-permute-start | bytes 294920 | tf_op jit(solution)/shard_map/ppermute | solution.py:219
  96.3 7.6 %collective-permute-start.47 = (f32[32,768]{1,0:T(8,128)S(1)}, f32[32,768]{1,0:T(8,128)S(1)}, u32[]{:S(2)}, u32[]{:S(2)}) collective-permute-start(f32[32,768]{1,0:T(8,128)S(1)} %shard_map.77.refs_12_), channel_id=1, source_target_pairs={{0,4},{1,5},{2,6},{3,7},{4,8},{5,9},{6,10},{7,11},{8,12},{9,13},{1... | collective-permute-start | bytes 294920 | tf_op jit(solution)/shard_map/ppermute | solution.py:219
  96.6 8.3 %collective-permute-start.58 = (f32[32,768]{1,0:T(8,128)S(1)}, f32[32,768]{1,0:T(8,128)S(1)}, u32[]{:S(2)}, u32[]{:S(2)}) collective-permute-start(f32[32,768]{1,0:T(8,128)S(1)} %shard_map.77.refs_12_), channel_id=1, source_target_pairs={{0,2},{1,3},{2,0},{3,1},{4,6},{5,7},{6,4},{7,5},{8,10},{9,11},{10,... | collective-permute-start | bytes 294920 | tf_op jit(solution)/shard_map/ppermute | solution.py:219
  97.7 12.0 %collective-permute-start.46 = (f32[32,768]{1,0:T(8,128)S(1)}, f32[32,768]{1,0:T(8,128)S(1)}, u32[]{:S(2)}, u32[]{:S(2)}) collective-permute-start(f32[32,768]{1,0:T(8,128)S(1)} %shard_map.77.refs_12_), channel_id=1, source_target_pairs={{0,10},{1,11},{2,8},{3,9},{4,14},{5,15},{6,12},{7,13},{8,2},{9,3},... | collective-permute-start | bytes 294920 | tf_op jit(solution)/shard_map/ppermute | solution.py:219
  98.4 12.9 %collective-permute-start.45 = (f32[32,768]{1,0:T(8,128)S(1)}, f32[32,768]{1,0:T(8,128)S(1)}, u32[]{:S(2)}, u32[]{:S(2)}) collective-permute-start(f32[32,768]{1,0:T(8,128)S(1)} %shard_map.77.refs_12_), channel_id=1, source_target_pairs={{0,8},{1,9},{2,10},{3,11},{4,12},{5,13},{6,14},{7,15},{8,0},{9,1},... | collective-permute-start | bytes 294920 | tf_op jit(solution)/shard_map/ppermute | solution.py:219
  101.0 10.2 %collective-permute-start.50 = (f32[32,768]{1,0:T(8,128)S(1)}, f32[32,768]{1,0:T(8,128)S(1)}, u32[]{:S(2)}, u32[]{:S(2)}) collective-permute-start(f32[32,768]{1,0:T(8,128)S(1)} %collective-permute-done.49.refs_4_), channel_id=1, source_target_pairs={{0,2},{1,3},{2,0},{3,1},{4,6},{5,7},{6,4},{7,5},{8,10},{9,11},{10,... | collective-permute-start | bytes 294920 | tf_op jit(solution)/shard_map/ppermute | solution.py:219
  103.8 7.9 %collective-permute-start.48 = (f32[32,768]{1,0:T(8,128)S(1)}, f32[32,768]{1,0:T(8,128)S(1)}, u32[]{:S(2)}, u32[]{:S(2)}) collective-permute-start(f32[32,768]{1,0:T(8,128)S(1)} %collective-permute-done.47.refs_8_), channel_id=1, source_target_pairs={{0,2},{1,3},{2,0},{3,1},{4,6},{5,7},{6,4},{7,5},{8,10},{9,11},{10,... | collective-permute-start | bytes 294920 | tf_op jit(solution)/shard_map/ppermute | solution.py:219
  104.9 6.9 %collective-permute-start.57 = (f32[32,768]{1,0:T(8,128)S(1)}, f32[32,768]{1,0:T(8,128)S(1)}, u32[]{:S(2)}, u32[]{:S(2)}) collective-permute-start(f32[32,768]{1,0:T(8,128)S(1)} %shard_map.77.refs_12_), channel_id=1, source_target_pairs={{0,1},{1,0},{2,3},{3,2},{4,5},{5,4},{6,7},{7,6},{8,9},{9,8},{10,11... | collective-permute-start | bytes 294920 | tf_op jit(solution)/shard_map/ppermute | solution.py:219
  121.4 6.5 %collective-permute-start.64 = (f32[32,768]{1,0:T(8,128)S(1)}, f32[32,768]{1,0:T(8,128)S(1)}, u32[]{:S(2)}, u32[]{:S(2)}) collective-permute-start(f32[32,768]{1,0:T(8,128)S(1)} %shard_map.79.refs_12_), channel_id=1, source_target_pairs={{0,12},{1,13},{2,14},{3,15},{4,0},{5,1},{6,2},{7,3},{8,4},{9,5},{1... | collective-permute-start | bytes 294920 | tf_op jit(solution)/shard_map/ppermute | solution.py:219
  123.2 7.6 %collective-permute-start.62 = (f32[32,768]{1,0:T(8,128)S(1)}, f32[32,768]{1,0:T(8,128)S(1)}, u32[]{:S(2)}, u32[]{:S(2)}) collective-permute-start(f32[32,768]{1,0:T(8,128)S(1)} %shard_map.79.refs_12_), channel_id=1, source_target_pairs={{0,4},{1,5},{2,6},{3,7},{4,8},{5,9},{6,10},{7,11},{8,12},{9,13},{1... | collective-permute-start | bytes 294920 | tf_op jit(solution)/shard_map/ppermute | solution.py:219
  123.5 8.2 %collective-permute-start.73 = (f32[32,768]{1,0:T(8,128)S(1)}, f32[32,768]{1,0:T(8,128)S(1)}, u32[]{:S(2)}, u32[]{:S(2)}) collective-permute-start(f32[32,768]{1,0:T(8,128)S(1)} %shard_map.79.refs_12_), channel_id=1, source_target_pairs={{0,2},{1,3},{2,0},{3,1},{4,6},{5,7},{6,4},{7,5},{8,10},{9,11},{10,... | collective-permute-start | bytes 294920 | tf_op jit(solution)/shard_map/ppermute | solution.py:219
  124.5 12.0 %collective-permute-start.61 = (f32[32,768]{1,0:T(8,128)S(1)}, f32[32,768]{1,0:T(8,128)S(1)}, u32[]{:S(2)}, u32[]{:S(2)}) collective-permute-start(f32[32,768]{1,0:T(8,128)S(1)} %shard_map.79.refs_12_), channel_id=1, source_target_pairs={{0,10},{1,11},{2,8},{3,9},{4,14},{5,15},{6,12},{7,13},{8,2},{9,3},... | collective-permute-start | bytes 294920 | tf_op jit(solution)/shard_map/ppermute | solution.py:219
  125.2 12.8 %collective-permute-start.60 = (f32[32,768]{1,0:T(8,128)S(1)}, f32[32,768]{1,0:T(8,128)S(1)}, u32[]{:S(2)}, u32[]{:S(2)}) collective-permute-start(f32[32,768]{1,0:T(8,128)S(1)} %shard_map.79.refs_12_), channel_id=1, source_target_pairs={{0,8},{1,9},{2,10},{3,11},{4,12},{5,13},{6,14},{7,15},{8,0},{9,1},... | collective-permute-start | bytes 294920 | tf_op jit(solution)/shard_map/ppermute | solution.py:219
  127.9 10.2 %collective-permute-start.65 = (f32[32,768]{1,0:T(8,128)S(1)}, f32[32,768]{1,0:T(8,128)S(1)}, u32[]{:S(2)}, u32[]{:S(2)}) collective-permute-start(f32[32,768]{1,0:T(8,128)S(1)} %collective-permute-done.64.refs_4_), channel_id=1, source_target_pairs={{0,2},{1,3},{2,0},{3,1},{4,6},{5,7},{6,4},{7,5},{8,10},{9,11},{10,... | collective-permute-start | bytes 294920 | tf_op jit(solution)/shard_map/ppermute | solution.py:219
  130.7 7.9 %collective-permute-start.63 = (f32[32,768]{1,0:T(8,128)S(1)}, f32[32,768]{1,0:T(8,128)S(1)}, u32[]{:S(2)}, u32[]{:S(2)}) collective-permute-start(f32[32,768]{1,0:T(8,128)S(1)} %collective-permute-done.62.refs_8_), channel_id=1, source_target_pairs={{0,2},{1,3},{2,0},{3,1},{4,6},{5,7},{6,4},{7,5},{8,10},{9,11},{10,... | collective-permute-start | bytes 294920 | tf_op jit(solution)/shard_map/ppermute | solution.py:219
  131.7 7.0 %collective-permute-start.72 = (f32[32,768]{1,0:T(8,128)S(1)}, f32[32,768]{1,0:T(8,128)S(1)}, u32[]{:S(2)}, u32[]{:S(2)}) collective-permute-start(f32[32,768]{1,0:T(8,128)S(1)} %shard_map.79.refs_12_), channel_id=1, source_target_pairs={{0,1},{1,0},{2,3},{3,2},{4,5},{5,4},{6,7},{7,6},{8,9},{9,8},{10,11... | collective-permute-start | bytes 294920 | tf_op jit(solution)/shard_map/ppermute | solution.py:219
  148.1 6.5 %collective-permute-start.79 = (f32[32,768]{1,0:T(8,128)S(1)}, f32[32,768]{1,0:T(8,128)S(1)}, u32[]{:S(2)}, u32[]{:S(2)}) collective-permute-start(f32[32,768]{1,0:T(8,128)S(1)} %shard_map.81.refs_12_), channel_id=1, source_target_pairs={{0,12},{1,13},{2,14},{3,15},{4,0},{5,1},{6,2},{7,3},{8,4},{9,5},{1... | collective-permute-start | bytes 294920 | tf_op jit(solution)/shard_map/ppermute | solution.py:219
  149.8 7.6 %collective-permute-start.77 = (f32[32,768]{1,0:T(8,128)S(1)}, f32[32,768]{1,0:T(8,128)S(1)}, u32[]{:S(2)}, u32[]{:S(2)}) collective-permute-start(f32[32,768]{1,0:T(8,128)S(1)} %shard_map.81.refs_12_), channel_id=1, source_target_pairs={{0,4},{1,5},{2,6},{3,7},{4,8},{5,9},{6,10},{7,11},{8,12},{9,13},{1... | collective-permute-start | bytes 294920 | tf_op jit(solution)/shard_map/ppermute | solution.py:219
  150.1 8.2 %collective-permute-start.88 = (f32[32,768]{1,0:T(8,128)S(1)}, f32[32,768]{1,0:T(8,128)S(1)}, u32[]{:S(2)}, u32[]{:S(2)}) collective-permute-start(f32[32,768]{1,0:T(8,128)S(1)} %shard_map.81.refs_12_), channel_id=1, source_target_pairs={{0,2},{1,3},{2,0},{3,1},{4,6},{5,7},{6,4},{7,5},{8,10},{9,11},{10,... | collective-permute-start | bytes 294920 | tf_op jit(solution)/shard_map/ppermute | solution.py:219
  151.2 12.0 %collective-permute-start.76 = (f32[32,768]{1,0:T(8,128)S(1)}, f32[32,768]{1,0:T(8,128)S(1)}, u32[]{:S(2)}, u32[]{:S(2)}) collective-permute-start(f32[32,768]{1,0:T(8,128)S(1)} %shard_map.81.refs_12_), channel_id=1, source_target_pairs={{0,10},{1,11},{2,8},{3,9},{4,14},{5,15},{6,12},{7,13},{8,2},{9,3},... | collective-permute-start | bytes 294920 | tf_op jit(solution)/shard_map/ppermute | solution.py:219
  151.9 12.8 %collective-permute-start.75 = (f32[32,768]{1,0:T(8,128)S(1)}, f32[32,768]{1,0:T(8,128)S(1)}, u32[]{:S(2)}, u32[]{:S(2)}) collective-permute-start(f32[32,768]{1,0:T(8,128)S(1)} %shard_map.81.refs_12_), channel_id=1, source_target_pairs={{0,8},{1,9},{2,10},{3,11},{4,12},{5,13},{6,14},{7,15},{8,0},{9,1},... | collective-permute-start | bytes 294920 | tf_op jit(solution)/shard_map/ppermute | solution.py:219
  154.5 10.2 %collective-permute-start.80 = (f32[32,768]{1,0:T(8,128)S(1)}, f32[32,768]{1,0:T(8,128)S(1)}, u32[]{:S(2)}, u32[]{:S(2)}) collective-permute-start(f32[32,768]{1,0:T(8,128)S(1)} %collective-permute-done.79.refs_4_), channel_id=1, source_target_pairs={{0,2},{1,3},{2,0},{3,1},{4,6},{5,7},{6,4},{7,5},{8,10},{9,11},{10,... | collective-permute-start | bytes 294920 | tf_op jit(solution)/shard_map/ppermute | solution.py:219
  157.4 7.9 %collective-permute-start.78 = (f32[32,768]{1,0:T(8,128)S(1)}, f32[32,768]{1,0:T(8,128)S(1)}, u32[]{:S(2)}, u32[]{:S(2)}) collective-permute-start(f32[32,768]{1,0:T(8,128)S(1)} %collective-permute-done.77.refs_8_), channel_id=1, source_target_pairs={{0,2},{1,3},{2,0},{3,1},{4,6},{5,7},{6,4},{7,5},{8,10},{9,11},{10,... | collective-permute-start | bytes 294920 | tf_op jit(solution)/shard_map/ppermute | solution.py:219
  158.4 7.0 %collective-permute-start.87 = (f32[32,768]{1,0:T(8,128)S(1)}, f32[32,768]{1,0:T(8,128)S(1)}, u32[]{:S(2)}, u32[]{:S(2)}) collective-permute-start(f32[32,768]{1,0:T(8,128)S(1)} %shard_map.81.refs_12_), channel_id=1, source_target_pairs={{0,1},{1,0},{2,3},{3,2},{4,5},{5,4},{6,7},{7,6},{8,9},{9,8},{10,11... | collective-permute-start | bytes 294920 | tf_op jit(solution)/shard_map/ppermute | solution.py:219
  177.3 5.4 %collective-permute-start.91 = (f32[2,16]{1,0:T(2,128)S(1)}, f32[2,16]{1,0:T(2,128)S(1)}, u32[]{:S(2)}, u32[]{:S(2)}) collective-permute-start(f32[2,16]{1,0:T(2,128)S(1)} %get-tuple-element.41), channel_id=1, source_target_pairs={{0,4},{1,5},{2,6},{3,7},{4,8},{5,9},{6,10},{7,11},{8,12},{9,13},{1... | collective-permute-start | bytes 392 | tf_op jit(solution)/shard_map/ppermute | solution.py:219
  177.6 5.0 %collective-permute-start.90 = (f32[2,16]{1,0:T(2,128)S(1)}, f32[2,16]{1,0:T(2,128)S(1)}, u32[]{:S(2)}, u32[]{:S(2)}) collective-permute-start(f32[2,16]{1,0:T(2,128)S(1)} %get-tuple-element.41), channel_id=1, source_target_pairs={{0,8},{1,9},{2,10},{3,11},{4,12},{5,13},{6,14},{7,15},{8,0},{9,1},... | collective-permute-start | bytes 392 | tf_op jit(solution)/shard_map/ppermute | solution.py:219
  (51 other events, 132.1 us)
where the time goes:
time: 188 us
  starting transfers between devices  67.5 us (36%)
  waiting for transfers between devices  60.6 us (32%)
  Pallas kernels  57.6 us (31%)
    ppermute x95, starting transfers between devices, move(): return lax.ppermute(x, 'body', pairs)  67.5 us
    ppermute x95, waiting for transfers between devices, move(): return lax.ppermute(x, 'body', pairs)  60.6 us
    pallas_call x6, Pallas kernels, sweep(): pl.pallas_call(functools.partial(sweep_kernel, heads, slots, places, last...  45.5 us
    pallas_call x1, Pallas kernels, body(): pl.pallas_call(near_kernel, in_specs=[HBM, VMEM], out_specs=[VMEM, VMEM],...  4.15 us
    pallas_call x1, Pallas kernels, body(): cross_b = split_late(all_blocks, same)  4.14 us
    pallas_call x1, Pallas kernels, body(): pl.pallas_call(functools.partial(first_kernel, heads), in_specs=[HBM, VME...  3.85 us
  transfers between devices with their start and end apart: 95, of which 46 were waited for; matrix products, arithmetic and copies ran while one was open for 0% of the time, Pallas kernels for 4%

commit v1 on v0

--- a/solution.py
+++ b/solution.py
@@ -249,12 +249,17 @@
             sources, part = sweep(True, *args, panel_weight)
         else:
             sources = sweep(False, *args)
-    terms = [part] + [move(part, z_pairs[d]) for d in range(1, lines)]
-    while len(terms) > 1:
-        half = len(terms) // 2
-        terms = [terms[i] + terms[i + half] for i in range(half)]
-    part = terms[0]
-    part = part + move(part, y_pairs)
+    lines_sum = []
+    for flip in (0, 2):
+        terms = []
+        for d in range(lines):
+            pairs = [(i, j ^ flip) for i, j in z_pairs[d]]
+            terms.append(move(part, pairs) if d or flip else part)
+        while len(terms) > 1:
+            half = len(terms) // 2
+            terms = [terms[i] + terms[i + half] for i in range(half)]
+        lines_sum.append(terms[0])
+    part = lines_sum[0] + lines_sum[1]
     part = part + move(part, c_pairs)
     return (sources.reshape(1, 2, heads, panels), part[None])
 

time: 188 us -> 190 us (1.011)
  starting transfers between devices: 67.5 us -> 74.1 us
  waiting for transfers between devices: 60.6 us -> 56.2 us
    ppermute x95 -> x98, starting transfers between devices: 67.5 us -> 74.1 us  [move(): return lax.ppermute(x, 'body', pairs)]
    ppermute x95 -> x98, waiting for transfers between devices: 60.6 us -> 56.2 us  [move(): return lax.ppermute(x, 'body', pairs)]
  transfers between devices with their start and end apart: 95 -> 98, of which waited for: 46 -> 45; matrix products, arithmetic and copies ran while one was open for 0% -> 0% of each run, Pallas kernels for 4% -> 4%
where the time goes in v1:
time: 190 us
  starting transfers between devices  74.1 us (39%)
  Pallas kernels  57.6 us (30%)
  waiting for transfers between devices  56.2 us (30%)
    ppermute x98, starting transfers between devices, move(): return lax.ppermute(x, 'body', pairs)  74.1 us
    ppermute x98, waiting for transfers between devices, move(): return lax.ppermute(x, 'body', pairs)  56.2 us
    pallas_call x6, Pallas kernels, sweep(): pl.pallas_call(functools.partial(sweep_kernel, heads, slots, places, last...  45.4 us
    pallas_call x1, Pallas kernels, body(): pl.pallas_call(near_kernel, in_specs=[HBM, VMEM], out_specs=[VMEM, VMEM],...  4.15 us
    pallas_call x1, Pallas kernels, body(): cross_b = split_late(all_blocks, same)  4.14 us
    pallas_call x1, Pallas kernels, body(): pl.pallas_call(functools.partial(first_kernel, heads), in_specs=[HBM, VME...  3.85 us
  transfers between devices with their start and end apart: 98, of which 45 were waited for; matrix products, arithmetic and copies ran while one was open for 0% of the time, Pallas kernels for 4%

profile of v1, /device:TPU:0, one launch (start us, length us, event | category | flops | bytes accessed | tf_op | source)
XLA Modules:
  0.0 190.3 jit_solution(13209029671035531902)
XLA Ops:
  1.5 3.9 %shard_map.68 = (bf16[3072,768]{1,0:T(8,128)(2,1)S(1)}, f32[32,768]{1,0:T(8,128)S(1)}) custom-call(f32[2,768,768]{2,1,0:T(8,128)} %bitcast.15, f32[32,768]{1,0:T(8,128)S(1)} %bitcast.6), custom_call_target="tpu_custom_call" | custom-call | tf_op jit(solution)/shard_map/pallas_call | solution.py:163
  5.4 3.0 %collective-permute-start.13 = (f32[32,768]{1,0:T(8,128)S(1)}, f32[32,768]{1,0:T(8,128)S(1)}, u32[]{:S(2)}, u32[]{:S(2)}) collective-permute-start(f32[32,768]{1,0:T(8,128)S(1)} %get-tuple-element.22.field_ref.refs_12_), channel_id=1, source_target_pairs={{0,2},{1,3},{2,0},{3,1},{4,6},{5,7},{6,4},{7,5},{8,10},{9,11},{10,... | collective-permute-start | bytes 294920 | tf_op jit(solution)/shard_map/ppermute | solution.py:219
  8.4 3.6 %collective-permute-start.3 = (f32[32,768]{1,0:T(8,128)S(1)}, f32[32,768]{1,0:T(8,128)S(1)}, u32[]{:S(2)}, u32[]{:S(2)}) collective-permute-start(f32[32,768]{1,0:T(8,128)S(1)} %get-tuple-element.22.field_ref.refs_12_), channel_id=1, source_target_pairs={{0,12},{1,13},{2,14},{3,15},{4,0},{5,1},{6,2},{7,3},{8,4},{9,5},{1... | collective-permute-start | bytes 294920 | tf_op jit(solution)/shard_map/ppermute | solution.py:219
  12.0 4.1 %shard_map.69 = (bf16[3072,1536]{1,0:T(8,128)(2,1)S(1)}, f32[32,768]{1,0:T(8,128)S(1)}) custom-call(f32[8,768,768]{2,1,0:T(8,128)} %bitcast.13, f32[32,768]{1,0:T(8,128)S(1)} %get-tuple-element.22.field_ref.refs_12_), custom_call_target="tpu_custom_call" | custom-call | flops 37748736 | bytes 9437184 | tf_op jit(solution)/shard_map/pallas_call | solution.py:185
  17.2 1.9 %collective-permute-start = (f32[32,768]{1,0:T(8,128)S(1)}, f32[32,768]{1,0:T(8,128)S(1)}, u32[]{:S(2)}, u32[]{:S(2)}) collective-permute-start(f32[32,768]{1,0:T(8,128)S(1)} %get-tuple-element.23.waited), channel_id=1, source_target_pairs={{0,8},{1,9},{2,10},{3,11},{4,12},{5,13},{6,14},{7,15},{8,0},{9,1},... | collective-permute-start | bytes 294920 | tf_op jit(solution)/shard_map/ppermute | solution.py:219
  19.1 4.1 %shard_map.70.refs_2_.refs_18_ = bf16[3072,1536]{1,0:T(8,128)(2,1)S(1)} custom-call(f32[8,768,768]{2,1,0:T(8,128)} %bitcast.14, f32[32,768]{1,0:T(8,128)S(1)} %get-tuple-element.23.waited), custom_call_target="tpu_custom_call" | custom-call | flops 37748736 | bytes 9437184 | tf_op jit(solution)/shard_map/pallas_call | solution.py:235
  23.3 1.6 collective-permute-start.4
  25.4 1.5 collective-permute-done.1.refs_1_
  28.4 1.1 collective-permute-done.5.refs_3_.refs_6_
  31.5 7.4 %shard_map.73.refs_12_ = f32[32,768]{1,0:T(8,128)S(1)} custom-call(s32[1,4]{1,0:T(1,128)S(1)} %copy-done.2, f32[32,768]{1,0:T(8,128)S(1)} %get-tuple-element.26.refs_0_, f32[32,768]{1,0:T(8,128)S(1)} %collective-permute-done.6.refs_1_, f32[32,768]{1,0:T(8,128)S(1)} %get-tuple-element.27.refs_2_, f32[32,768]{1,0:T(8,128)S(1)} %collective-permute-done.7.refs_3_, ...), custom_call_target="tpu_custom_call" | custom-call | tf_op jit(solution)/shard_map/pallas_call | solution.py:205
  38.9 3.9 %collective-permute-start.19 = (f32[32,768]{1,0:T(8,128)S(1)}, f32[32,768]{1,0:T(8,128)S(1)}, u32[]{:S(2)}, u32[]{:S(2)}) collective-permute-start(f32[32,768]{1,0:T(8,128)S(1)} %shard_map.73.refs_12_), channel_id=1, source_target_pairs={{0,12},{1,13},{2,14},{3,15},{4,0},{5,1},{6,2},{7,3},{8,4},{9,5},{1... | collective-permute-start | bytes 294920 | tf_op jit(solution)/shard_map/ppermute | solution.py:219
  44.8 2.3 %collective-permute-start.15 = (f32[32,768]{1,0:T(8,128)S(1)}, f32[32,768]{1,0:T(8,128)S(1)}, u32[]{:S(2)}, u32[]{:S(2)}) collective-permute-start(f32[32,768]{1,0:T(8,128)S(1)} %shard_map.73.refs_12_), channel_id=1, source_target_pairs={{0,8},{1,9},{2,10},{3,11},{4,12},{5,13},{6,14},{7,15},{8,0},{9,1},... | collective-permute-start | bytes 294920 | tf_op jit(solution)/shard_map/ppermute | solution.py:219
  48.2 2.1 %collective-permute-done.17.refs_8_ = f32[32,768]{1,0:T(8,128)S(1)} collective-permute-done((f32[32,768]{1,0:T(8,128)S(1)}, f32[32,768]{1,0:T(8,128)S(1)}, u32[]{:S(2)}, u32[]{:S(2)}) %collective-permute-start.17) | collective-permute-done | bytes 98336 | tf_op jit(solution)/shard_map/ppermute | solution.py:219
  51.4 4.9 %collective-permute-done.16.refs_1_ = f32[32,768]{1,0:T(8,128)S(1)} collective-permute-done((f32[32,768]{1,0:T(8,128)S(1)}, f32[32,768]{1,0:T(8,128)S(1)}, u32[]{:S(2)}, u32[]{:S(2)}) %collective-permute-start.16) | collective-permute-done | bytes 98336 | tf_op jit(solution)/shard_map/ppermute | solution.py:219
  56.3 1.5 collective-permute-done.15.refs_0_
  60.4 7.5 %shard_map.75.refs_12_ = f32[32,768]{1,0:T(8,128)S(1)} custom-call(s32[1,4]{1,0:T(1,128)S(1)} %copy-done.2, f32[32,768]{1,0:T(8,128)S(1)} %get-tuple-element.30.refs_0_, f32[32,768]{1,0:T(8,128)S(1)} %collective-permute-done.21.refs_1_, f32[32,768]{1,0:T(8,128)S(1)} %get-tuple-element.31.refs_2_, f32[32,768]{1,0:T(8,128)S(1)} %collective-permute-done.22.refs_3_, ...), custom_call_target="tpu_custom_call" | custom-call | tf_op jit(solution)/shard_map/pallas_call | solution.py:205
  67.9 1.7 collective-permute-start.34
  70.0 1.1 collective-permute-start.43
  71.8 2.6 %collective-permute-start.30 = (f32[32,768]{1,0:T(8,128)S(1)}, f32[32,768]{1,0:T(8,128)S(1)}, u32[]{:S(2)}, u32[]{:S(2)}) collective-permute-start(f32[32,768]{1,0:T(8,128)S(1)} %shard_map.75.refs_12_), channel_id=1, source_target_pairs={{0,8},{1,9},{2,10},{3,11},{4,12},{5,13},{6,14},{7,15},{8,0},{9,1},... | collective-permute-start | bytes 294920 | tf_op jit(solution)/shard_map/ppermute | solution.py:219
  74.4 1.1 collective-permute-start.35
  75.5 1.8 collective-permute-done.32.refs_8_
  78.3 4.8 %collective-permute-done.31.refs_1_ = f32[32,768]{1,0:T(8,128)S(1)} collective-permute-done((f32[32,768]{1,0:T(8,128)S(1)}, f32[32,768]{1,0:T(8,128)S(1)}, u32[]{:S(2)}, u32[]{:S(2)}) %collective-permute-start.31) | collective-permute-done | bytes 98336 | tf_op jit(solution)/shard_map/ppermute | solution.py:219
  83.1 1.5 collective-permute-done.30.refs_0_
  87.2 7.3 %shard_map.77.refs_12_ = f32[32,768]{1,0:T(8,128)S(1)} custom-call(s32[1,4]{1,0:T(1,128)S(1)} %copy-done.2, f32[32,768]{1,0:T(8,128)S(1)} %get-tuple-element.32.refs_0_, f32[32,768]{1,0:T(8,128)S(1)} %collective-permute-done.36.refs_1_, f32[32,768]{1,0:T(8,128)S(1)} %get-tuple-element.33.refs_2_, f32[32,768]{1,0:T(8,128)S(1)} %collective-permute-done.37.refs_3_, ...), custom_call_target="tpu_custom_call" | custom-call | tf_op jit(solution)/shard_map/pallas_call | solution.py:205
  94.5 1.7 collective-permute-start.49
  98.4 2.6 %collective-permute-start.45 = (f32[32,768]{1,0:T(8,128)S(1)}, f32[32,768]{1,0:T(8,128)S(1)}, u32[]{:S(2)}, u32[]{:S(2)}) collective-permute-start(f32[32,768]{1,0:T(8,128)S(1)} %shard_map.77.refs_12_), channel_id=1, source_target_pairs={{0,8},{1,9},{2,10},{3,11},{4,12},{5,13},{6,14},{7,15},{8,0},{9,1},... | collective-permute-start | bytes 294920 | tf_op jit(solution)/shard_map/ppermute | solution.py:219
  102.1 1.8 collective-permute-done.47.refs_8_
  104.9 4.8 %collective-permute-done.46.refs_1_ = f32[32,768]{1,0:T(8,128)S(1)} collective-permute-done((f32[32,768]{1,0:T(8,128)S(1)}, f32[32,768]{1,0:T(8,128)S(1)}, u32[]{:S(2)}, u32[]{:S(2)}) %collective-permute-start.46) | collective-permute-done | bytes 98336 | tf_op jit(solution)/shard_map/ppermute | solution.py:219
  109.7 1.5 collective-permute-done.45.refs_0_
  113.8 7.6 %shard_map.79.refs_12_ = f32[32,768]{1,0:T(8,128)S(1)} custom-call(s32[1,4]{1,0:T(1,128)S(1)} %copy-done.2, f32[32,768]{1,0:T(8,128)S(1)} %get-tuple-element.34.refs_0_, f32[32,768]{1,0:T(8,128)S(1)} %collective-permute-done.51.refs_1_, f32[32,768]{1,0:T(8,128)S(1)} %get-tuple-element.35.refs_2_, f32[32,768]{1,0:T(8,128)S(1)} %collective-permute-done.52.refs_3_, ...), custom_call_target="tpu_custom_call" | custom-call | tf_op jit(solution)/shard_map/pallas_call | solution.py:205
  121.4 1.7 collective-permute-start.64
  125.2 2.6 %collective-permute-start.60 = (f32[32,768]{1,0:T(8,128)S(1)}, f32[32,768]{1,0:T(8,128)S(1)}, u32[]{:S(2)}, u32[]{:S(2)}) collective-permute-start(f32[32,768]{1,0:T(8,128)S(1)} %shard_map.79.refs_12_), channel_id=1, source_target_pairs={{0,8},{1,9},{2,10},{3,11},{4,12},{5,13},{6,14},{7,15},{8,0},{9,1},... | collective-permute-start | bytes 294920 | tf_op jit(solution)/shard_map/ppermute | solution.py:219
  127.9 1.1 collective-permute-start.65
  128.9 1.8 collective-permute-done.62.refs_8_
  131.7 4.8 %collective-permute-done.61.refs_1_ = f32[32,768]{1,0:T(8,128)S(1)} collective-permute-done((f32[32,768]{1,0:T(8,128)S(1)}, f32[32,768]{1,0:T(8,128)S(1)}, u32[]{:S(2)}, u32[]{:S(2)}) %collective-permute-start.61) | collective-permute-done | bytes 98336 | tf_op jit(solution)/shard_map/ppermute | solution.py:219
  136.6 1.5 collective-permute-done.60.refs_0_
  140.7 7.4 %shard_map.81.refs_12_ = f32[32,768]{1,0:T(8,128)S(1)} custom-call(s32[1,4]{1,0:T(1,128)S(1)} %copy-done.2, f32[32,768]{1,0:T(8,128)S(1)} %get-tuple-element.36.refs_0_, f32[32,768]{1,0:T(8,128)S(1)} %collective-permute-done.66.refs_1_, f32[32,768]{1,0:T(8,128)S(1)} %get-tuple-element.37.refs_2_, f32[32,768]{1,0:T(8,128)S(1)} %collective-permute-done.67.refs_3_, ...), custom_call_target="tpu_custom_call" | custom-call | tf_op jit(solution)/shard_map/pallas_call | solution.py:205
  148.0 1.7 collective-permute-start.79
  151.9 2.7 %collective-permute-start.75 = (f32[32,768]{1,0:T(8,128)S(1)}, f32[32,768]{1,0:T(8,128)S(1)}, u32[]{:S(2)}, u32[]{:S(2)}) collective-permute-start(f32[32,768]{1,0:T(8,128)S(1)} %shard_map.81.refs_12_), channel_id=1, source_target_pairs={{0,8},{1,9},{2,10},{3,11},{4,12},{5,13},{6,14},{7,15},{8,0},{9,1},... | collective-permute-start | bytes 294920 | tf_op jit(solution)/shard_map/ppermute | solution.py:219
  155.6 1.8 collective-permute-done.77.refs_8_
  158.4 4.8 %collective-permute-done.76.refs_1_ = f32[32,768]{1,0:T(8,128)S(1)} collective-permute-done((f32[32,768]{1,0:T(8,128)S(1)}, f32[32,768]{1,0:T(8,128)S(1)}, u32[]{:S(2)}, u32[]{:S(2)}) %collective-permute-start.76) | collective-permute-done | bytes 98336 | tf_op jit(solution)/shard_map/ppermute | solution.py:219
  163.2 1.5 collective-permute-done.75.refs_0_
  167.3 8.3 %shard_map.83 = (f32[32,768]{1,0:T(8,128)}, f32[2,16]{1,0:T(2,128)S(1)}) custom-call(s32[1,4]{1,0:T(1,128)S(1)} %copy-done.2, f32[32,768]{1,0:T(8,128)S(1)} %get-tuple-element.38.refs_0_, f32[32,768]{1,0:T(8,128)S(1)} %collective-permute-done.81.refs_1_, f32[32,768]{1,0:T(8,128)S(1)} %get-tuple-element.39.refs_2_, ...), custom_call_target="tpu_custom_call" | custom-call | tf_op jit(solution)/shard_map/pallas_call | solution.py:205
  175.6 2.1 %collective-permute-start.96 = (f32[2,16]{1,0:T(2,128)S(1)}, f32[2,16]{1,0:T(2,128)S(1)}, u32[]{:S(2)}, u32[]{:S(2)}) collective-permute-start(f32[2,16]{1,0:T(2,128)S(1)} %get-tuple-element.41), channel_id=1, source_target_pairs={{0,14},{1,15},{2,12},{3,13},{4,2},{5,3},{6,0},{7,1},{8,6},{9,7},{1... | collective-permute-start | bytes 392 | tf_op jit(solution)/shard_map/ppermute | solution.py:219
  179.8 3.3 %collective-permute-start.92 = (f32[2,16]{1,0:T(2,128)S(1)}, f32[2,16]{1,0:T(2,128)S(1)}, u32[]{:S(2)}, u32[]{:S(2)}) collective-permute-start(f32[2,16]{1,0:T(2,128)S(1)} %get-tuple-element.41), channel_id=1, source_target_pairs={{0,12},{1,13},{2,14},{3,15},{4,0},{5,1},{6,2},{7,3},{8,4},{9,5},{1... | collective-permute-start | bytes 392 | tf_op jit(solution)/shard_map/ppermute | solution.py:219
  184.0 1.5 collective-permute-start.90
  185.6 2.8 %collective-permute-done.91 = f32[2,16]{1,0:T(2,128)S(1)} collective-permute-done((f32[2,16]{1,0:T(2,128)S(1)}, f32[2,16]{1,0:T(2,128)S(1)}, u32[]{:S(2)}, u32[]{:S(2)}) %collective-permute-start.91) | collective-permute-done | bytes 160 | tf_op jit(solution)/shard_map/ppermute | solution.py:219
  188.6 1.1 collective-permute-done.97
  (174 shorter events, 40.4 us)
Async XLA Ops:
  5.4 20.0 %collective-permute-start.13 = (f32[32,768]{1,0:T(8,128)S(1)}, f32[32,768]{1,0:T(8,128)S(1)}, u32[]{:S(2)}, u32[]{:S(2)}) collective-permute-start(f32[32,768]{1,0:T(8,128)S(1)} %get-tuple-element.22.field_ref.refs_12_), channel_id=1, source_target_pairs={{0,2},{1,3},{2,0},{3,1},{4,6},{5,7},{6,4},{7,5},{8,10},{9,11},{10,... | collective-permute-start | bytes 294920 | tf_op jit(solution)/shard_map/ppermute | solution.py:219
  8.4 14.9 %collective-permute-start.3 = (f32[32,768]{1,0:T(8,128)S(1)}, f32[32,768]{1,0:T(8,128)S(1)}, u32[]{:S(2)}, u32[]{:S(2)}) collective-permute-start(f32[32,768]{1,0:T(8,128)S(1)} %get-tuple-element.22.field_ref.refs_12_), channel_id=1, source_target_pairs={{0,12},{1,13},{2,14},{3,15},{4,0},{5,1},{6,2},{7,3},{8,4},{9,5},{1... | collective-permute-start | bytes 294920 | tf_op jit(solution)/shard_map/ppermute | solution.py:219
  12.0 11.3 %collective-permute-start.2 = (f32[32,768]{1,0:T(8,128)S(1)}, f32[32,768]{1,0:T(8,128)S(1)}, u32[]{:S(2)}, u32[]{:S(2)}) collective-permute-start(f32[32,768]{1,0:T(8,128)S(1)} %get-tuple-element.22.field_ref.refs_12_), channel_id=1, source_target_pairs={{0,4},{1,5},{2,6},{3,7},{4,8},{5,9},{6,10},{7,11},{8,12},{9,13},{1... | collective-permute-start | bytes 294920 | tf_op jit(solution)/shard_map/ppermute | solution.py:219
  16.2 10.7 %collective-permute-start.1 = (f32[32,768]{1,0:T(8,128)S(1)}, f32[32,768]{1,0:T(8,128)S(1)}, u32[]{:S(2)}, u32[]{:S(2)}) collective-permute-start(f32[32,768]{1,0:T(8,128)S(1)} %get-tuple-element.23.waited), channel_id=1, source_target_pairs={{0,10},{1,11},{2,8},{3,9},{4,14},{5,15},{6,12},{7,13},{8,2},{9,3},... | collective-permute-start | bytes 294920 | tf_op jit(solution)/shard_map/ppermute | solution.py:219
  17.2 10.2 %collective-permute-start = (f32[32,768]{1,0:T(8,128)S(1)}, f32[32,768]{1,0:T(8,128)S(1)}, u32[]{:S(2)}, u32[]{:S(2)}) collective-permute-start(f32[32,768]{1,0:T(8,128)S(1)} %get-tuple-element.23.waited), channel_id=1, source_target_pairs={{0,8},{1,9},{2,10},{3,11},{4,12},{5,13},{6,14},{7,15},{8,0},{9,1},... | collective-permute-start | bytes 294920 | tf_op jit(solution)/shard_map/ppermute | solution.py:219
  38.9 8.3 %collective-permute-start.19 = (f32[32,768]{1,0:T(8,128)S(1)}, f32[32,768]{1,0:T(8,128)S(1)}, u32[]{:S(2)}, u32[]{:S(2)}) collective-permute-start(f32[32,768]{1,0:T(8,128)S(1)} %shard_map.73.refs_12_), channel_id=1, source_target_pairs={{0,12},{1,13},{2,14},{3,15},{4,0},{5,1},{6,2},{7,3},{8,4},{9,5},{1... | collective-permute-start | bytes 294920 | tf_op jit(solution)/shard_map/ppermute | solution.py:219
  42.8 7.5 %collective-permute-start.17 = (f32[32,768]{1,0:T(8,128)S(1)}, f32[32,768]{1,0:T(8,128)S(1)}, u32[]{:S(2)}, u32[]{:S(2)}) collective-permute-start(f32[32,768]{1,0:T(8,128)S(1)} %shard_map.73.refs_12_), channel_id=1, source_target_pairs={{0,4},{1,5},{2,6},{3,7},{4,8},{5,9},{6,10},{7,11},{8,12},{9,13},{1... | collective-permute-start | bytes 294920 | tf_op jit(solution)/shard_map/ppermute | solution.py:219
  42.8 8.6 %collective-permute-start.28 = (f32[32,768]{1,0:T(8,128)S(1)}, f32[32,768]{1,0:T(8,128)S(1)}, u32[]{:S(2)}, u32[]{:S(2)}) collective-permute-start(f32[32,768]{1,0:T(8,128)S(1)} %shard_map.73.refs_12_), channel_id=1, source_target_pairs={{0,2},{1,3},{2,0},{3,1},{4,6},{5,7},{6,4},{7,5},{8,10},{9,11},{10,... | collective-permute-start | bytes 294920 | tf_op jit(solution)/shard_map/ppermute | solution.py:219
  43.8 12.5 %collective-permute-start.16 = (f32[32,768]{1,0:T(8,128)S(1)}, f32[32,768]{1,0:T(8,128)S(1)}, u32[]{:S(2)}, u32[]{:S(2)}) collective-permute-start(f32[32,768]{1,0:T(8,128)S(1)} %shard_map.73.refs_12_), channel_id=1, source_target_pairs={{0,10},{1,11},{2,8},{3,9},{4,14},{5,15},{6,12},{7,13},{8,2},{9,3},... | collective-permute-start | bytes 294920 | tf_op jit(solution)/shard_map/ppermute | solution.py:219
  44.8 12.9 %collective-permute-start.15 = (f32[32,768]{1,0:T(8,128)S(1)}, f32[32,768]{1,0:T(8,128)S(1)}, u32[]{:S(2)}, u32[]{:S(2)}) collective-permute-start(f32[32,768]{1,0:T(8,128)S(1)} %shard_map.73.refs_12_), channel_id=1, source_target_pairs={{0,8},{1,9},{2,10},{3,11},{4,12},{5,13},{6,14},{7,15},{8,0},{9,1},... | collective-permute-start | bytes 294920 | tf_op jit(solution)/shard_map/ppermute | solution.py:219
  47.1 10.6 %collective-permute-start.20 = (f32[32,768]{1,0:T(8,128)S(1)}, f32[32,768]{1,0:T(8,128)S(1)}, u32[]{:S(2)}, u32[]{:S(2)}) collective-permute-start(f32[32,768]{1,0:T(8,128)S(1)} %collective-permute-done.19.refs_4_), channel_id=1, source_target_pairs={{0,2},{1,3},{2,0},{3,1},{4,6},{5,7},{6,4},{7,5},{8,10},{9,11},{10,... | collective-permute-start | bytes 294920 | tf_op jit(solution)/shard_map/ppermute | solution.py:219
  50.3 8.0 %collective-permute-start.18 = (f32[32,768]{1,0:T(8,128)S(1)}, f32[32,768]{1,0:T(8,128)S(1)}, u32[]{:S(2)}, u32[]{:S(2)}) collective-permute-start(f32[32,768]{1,0:T(8,128)S(1)} %collective-permute-done.17.refs_8_), channel_id=1, source_target_pairs={{0,2},{1,3},{2,0},{3,1},{4,6},{5,7},{6,4},{7,5},{8,10},{9,11},{10,... | collective-permute-start | bytes 294920 | tf_op jit(solution)/shard_map/ppermute | solution.py:219
  51.4 7.0 %collective-permute-start.27 = (f32[32,768]{1,0:T(8,128)S(1)}, f32[32,768]{1,0:T(8,128)S(1)}, u32[]{:S(2)}, u32[]{:S(2)}) collective-permute-start(f32[32,768]{1,0:T(8,128)S(1)} %shard_map.73.refs_12_), channel_id=1, source_target_pairs={{0,1},{1,0},{2,3},{3,2},{4,5},{5,4},{6,7},{7,6},{8,9},{9,8},{10,11... | collective-permute-start | bytes 294920 | tf_op jit(solution)/shard_map/ppermute | solution.py:219
  67.9 6.5 %collective-permute-start.34 = (f32[32,768]{1,0:T(8,128)S(1)}, f32[32,768]{1,0:T(8,128)S(1)}, u32[]{:S(2)}, u32[]{:S(2)}) collective-permute-start(f32[32,768]{1,0:T(8,128)S(1)} %shard_map.75.refs_12_), channel_id=1, source_target_pairs={{0,12},{1,13},{2,14},{3,15},{4,0},{5,1},{6,2},{7,3},{8,4},{9,5},{1... | collective-permute-start | bytes 294920 | tf_op jit(solution)/shard_map/ppermute | solution.py:219
  69.7 7.6 %collective-permute-start.32 = (f32[32,768]{1,0:T(8,128)S(1)}, f32[32,768]{1,0:T(8,128)S(1)}, u32[]{:S(2)}, u32[]{:S(2)}) collective-permute-start(f32[32,768]{1,0:T(8,128)S(1)} %shard_map.75.refs_12_), channel_id=1, source_target_pairs={{0,4},{1,5},{2,6},{3,7},{4,8},{5,9},{6,10},{7,11},{8,12},{9,13},{1... | collective-permute-start | bytes 294920 | tf_op jit(solution)/shard_map/ppermute | solution.py:219
  70.0 8.3 %collective-permute-start.43 = (f32[32,768]{1,0:T(8,128)S(1)}, f32[32,768]{1,0:T(8,128)S(1)}, u32[]{:S(2)}, u32[]{:S(2)}) collective-permute-start(f32[32,768]{1,0:T(8,128)S(1)} %shard_map.75.refs_12_), channel_id=1, source_target_pairs={{0,2},{1,3},{2,0},{3,1},{4,6},{5,7},{6,4},{7,5},{8,10},{9,11},{10,... | collective-permute-start | bytes 294920 | tf_op jit(solution)/shard_map/ppermute | solution.py:219
  71.1 12.0 %collective-permute-start.31 = (f32[32,768]{1,0:T(8,128)S(1)}, f32[32,768]{1,0:T(8,128)S(1)}, u32[]{:S(2)}, u32[]{:S(2)}) collective-permute-start(f32[32,768]{1,0:T(8,128)S(1)} %shard_map.75.refs_12_), channel_id=1, source_target_pairs={{0,10},{1,11},{2,8},{3,9},{4,14},{5,15},{6,12},{7,13},{8,2},{9,3},... | collective-permute-start | bytes 294920 | tf_op jit(solution)/shard_map/ppermute | solution.py:219
  71.8 12.8 %collective-permute-start.30 = (f32[32,768]{1,0:T(8,128)S(1)}, f32[32,768]{1,0:T(8,128)S(1)}, u32[]{:S(2)}, u32[]{:S(2)}) collective-permute-start(f32[32,768]{1,0:T(8,128)S(1)} %shard_map.75.refs_12_), channel_id=1, source_target_pairs={{0,8},{1,9},{2,10},{3,11},{4,12},{5,13},{6,14},{7,15},{8,0},{9,1},... | collective-permute-start | bytes 294920 | tf_op jit(solution)/shard_map/ppermute | solution.py:219
  74.4 10.2 %collective-permute-start.35 = (f32[32,768]{1,0:T(8,128)S(1)}, f32[32,768]{1,0:T(8,128)S(1)}, u32[]{:S(2)}, u32[]{:S(2)}) collective-permute-start(f32[32,768]{1,0:T(8,128)S(1)} %collective-permute-done.34.refs_4_), channel_id=1, source_target_pairs={{0,2},{1,3},{2,0},{3,1},{4,6},{5,7},{6,4},{7,5},{8,10},{9,11},{10,... | collective-permute-start | bytes 294920 | tf_op jit(solution)/shard_map/ppermute | solution.py:219
  77.2 7.9 %collective-permute-start.33 = (f32[32,768]{1,0:T(8,128)S(1)}, f32[32,768]{1,0:T(8,128)S(1)}, u32[]{:S(2)}, u32[]{:S(2)}) collective-permute-start(f32[32,768]{1,0:T(8,128)S(1)} %collective-permute-done.32.refs_8_), channel_id=1, source_target_pairs={{0,2},{1,3},{2,0},{3,1},{4,6},{5,7},{6,4},{7,5},{8,10},{9,11},{10,... | collective-permute-start | bytes 294920 | tf_op jit(solution)/shard_map/ppermute | solution.py:219
  78.3 6.9 %collective-permute-start.42 = (f32[32,768]{1,0:T(8,128)S(1)}, f32[32,768]{1,0:T(8,128)S(1)}, u32[]{:S(2)}, u32[]{:S(2)}) collective-permute-start(f32[32,768]{1,0:T(8,128)S(1)} %shard_map.75.refs_12_), channel_id=1, source_target_pairs={{0,1},{1,0},{2,3},{3,2},{4,5},{5,4},{6,7},{7,6},{8,9},{9,8},{10,11... | collective-permute-start | bytes 294920 | tf_op jit(solution)/shard_map/ppermute | solution.py:219
  94.5 6.5 %collective-permute-start.49 = (f32[32,768]{1,0:T(8,128)S(1)}, f32[32,768]{1,0:T(8,128)S(1)}, u32[]{:S(2)}, u32[]{:S(2)}) collective-permute-start(f32[32,768]{1,0:T(8,128)S(1)} %shard_map.77.refs_12_), channel_id=1, source_target_pairs={{0,12},{1,13},{2,14},{3,15},{4,0},{5,1},{6,2},{7,3},{8,4},{9,5},{1... | collective-permute-start | bytes 294920 | tf_op jit(solution)/shard_map/ppermute | solution.py:219
  96.3 7.6 %collective-permute-start.47 = (f32[32,768]{1,0:T(8,128)S(1)}, f32[32,768]{1,0:T(8,128)S(1)}, u32[]{:S(2)}, u32[]{:S(2)}) collective-permute-start(f32[32,768]{1,0:T(8,128)S(1)} %shard_map.77.refs_12_), channel_id=1, source_target_pairs={{0,4},{1,5},{2,6},{3,7},{4,8},{5,9},{6,10},{7,11},{8,12},{9,13},{1... | collective-permute-start | bytes 294920 | tf_op jit(solution)/shard_map/ppermute | solution.py:219
  96.6 8.3 %collective-permute-start.58 = (f32[32,768]{1,0:T(8,128)S(1)}, f32[32,768]{1,0:T(8,128)S(1)}, u32[]{:S(2)}, u32[]{:S(2)}) collective-permute-start(f32[32,768]{1,0:T(8,128)S(1)} %shard_map.77.refs_12_), channel_id=1, source_target_pairs={{0,2},{1,3},{2,0},{3,1},{4,6},{5,7},{6,4},{7,5},{8,10},{9,11},{10,... | collective-permute-start | bytes 294920 | tf_op jit(solution)/shard_map/ppermute | solution.py:219
  97.7 12.0 %collective-permute-start.46 = (f32[32,768]{1,0:T(8,128)S(1)}, f32[32,768]{1,0:T(8,128)S(1)}, u32[]{:S(2)}, u32[]{:S(2)}) collective-permute-start(f32[32,768]{1,0:T(8,128)S(1)} %shard_map.77.refs_12_), channel_id=1, source_target_pairs={{0,10},{1,11},{2,8},{3,9},{4,14},{5,15},{6,12},{7,13},{8,2},{9,3},... | collective-permute-start | bytes 294920 | tf_op jit(solution)/shard_map/ppermute | solution.py:219
  98.4 12.8 %collective-permute-start.45 = (f32[32,768]{1,0:T(8,128)S(1)}, f32[32,768]{1,0:T(8,128)S(1)}, u32[]{:S(2)}, u32[]{:S(2)}) collective-permute-start(f32[32,768]{1,0:T(8,128)S(1)} %shard_map.77.refs_12_), channel_id=1, source_target_pairs={{0,8},{1,9},{2,10},{3,11},{4,12},{5,13},{6,14},{7,15},{8,0},{9,1},... | collective-permute-start | bytes 294920 | tf_op jit(solution)/shard_map/ppermute | solution.py:219
  101.0 10.2 %collective-permute-start.50 = (f32[32,768]{1,0:T(8,128)S(1)}, f32[32,768]{1,0:T(8,128)S(1)}, u32[]{:S(2)}, u32[]{:S(2)}) collective-permute-start(f32[32,768]{1,0:T(8,128)S(1)} %collective-permute-done.49.refs_4_), channel_id=1, source_target_pairs={{0,2},{1,3},{2,0},{3,1},{4,6},{5,7},{6,4},{7,5},{8,10},{9,11},{10,... | collective-permute-start | bytes 294920 | tf_op jit(solution)/shard_map/ppermute | solution.py:219
  103.9 7.9 %collective-permute-start.48 = (f32[32,768]{1,0:T(8,128)S(1)}, f32[32,768]{1,0:T(8,128)S(1)}, u32[]{:S(2)}, u32[]{:S(2)}) collective-permute-start(f32[32,768]{1,0:T(8,128)S(1)} %collective-permute-done.47.refs_8_), channel_id=1, source_target_pairs={{0,2},{1,3},{2,0},{3,1},{4,6},{5,7},{6,4},{7,5},{8,10},{9,11},{10,... | collective-permute-start | bytes 294920 | tf_op jit(solution)/shard_map/ppermute | solution.py:219
  104.9 6.9 %collective-permute-start.57 = (f32[32,768]{1,0:T(8,128)S(1)}, f32[32,768]{1,0:T(8,128)S(1)}, u32[]{:S(2)}, u32[]{:S(2)}) collective-permute-start(f32[32,768]{1,0:T(8,128)S(1)} %shard_map.77.refs_12_), channel_id=1, source_target_pairs={{0,1},{1,0},{2,3},{3,2},{4,5},{5,4},{6,7},{7,6},{8,9},{9,8},{10,11... | collective-permute-start | bytes 294920 | tf_op jit(solution)/shard_map/ppermute | solution.py:219
  121.4 6.5 %collective-permute-start.64 = (f32[32,768]{1,0:T(8,128)S(1)}, f32[32,768]{1,0:T(8,128)S(1)}, u32[]{:S(2)}, u32[]{:S(2)}) collective-permute-start(f32[32,768]{1,0:T(8,128)S(1)} %shard_map.79.refs_12_), channel_id=1, source_target_pairs={{0,12},{1,13},{2,14},{3,15},{4,0},{5,1},{6,2},{7,3},{8,4},{9,5},{1... | collective-permute-start | bytes 294920 | tf_op jit(solution)/shard_map/ppermute | solution.py:219
  123.1 7.6 %collective-permute-start.62 = (f32[32,768]{1,0:T(8,128)S(1)}, f32[32,768]{1,0:T(8,128)S(1)}, u32[]{:S(2)}, u32[]{:S(2)}) collective-permute-start(f32[32,768]{1,0:T(8,128)S(1)} %shard_map.79.refs_12_), channel_id=1, source_target_pairs={{0,4},{1,5},{2,6},{3,7},{4,8},{5,9},{6,10},{7,11},{8,12},{9,13},{1... | collective-permute-start | bytes 294920 | tf_op jit(solution)/shard_map/ppermute | solution.py:219
  123.5 8.2 %collective-permute-start.73 = (f32[32,768]{1,0:T(8,128)S(1)}, f32[32,768]{1,0:T(8,128)S(1)}, u32[]{:S(2)}, u32[]{:S(2)}) collective-permute-start(f32[32,768]{1,0:T(8,128)S(1)} %shard_map.79.refs_12_), channel_id=1, source_target_pairs={{0,2},{1,3},{2,0},{3,1},{4,6},{5,7},{6,4},{7,5},{8,10},{9,11},{10,... | collective-permute-start | bytes 294920 | tf_op jit(solution)/shard_map/ppermute | solution.py:219
  124.5 12.0 %collective-permute-start.61 = (f32[32,768]{1,0:T(8,128)S(1)}, f32[32,768]{1,0:T(8,128)S(1)}, u32[]{:S(2)}, u32[]{:S(2)}) collective-permute-start(f32[32,768]{1,0:T(8,128)S(1)} %shard_map.79.refs_12_), channel_id=1, source_target_pairs={{0,10},{1,11},{2,8},{3,9},{4,14},{5,15},{6,12},{7,13},{8,2},{9,3},... | collective-permute-start | bytes 294920 | tf_op jit(solution)/shard_map/ppermute | solution.py:219
  125.2 12.8 %collective-permute-start.60 = (f32[32,768]{1,0:T(8,128)S(1)}, f32[32,768]{1,0:T(8,128)S(1)}, u32[]{:S(2)}, u32[]{:S(2)}) collective-permute-start(f32[32,768]{1,0:T(8,128)S(1)} %shard_map.79.refs_12_), channel_id=1, source_target_pairs={{0,8},{1,9},{2,10},{3,11},{4,12},{5,13},{6,14},{7,15},{8,0},{9,1},... | collective-permute-start | bytes 294920 | tf_op jit(solution)/shard_map/ppermute | solution.py:219
  127.9 10.2 %collective-permute-start.65 = (f32[32,768]{1,0:T(8,128)S(1)}, f32[32,768]{1,0:T(8,128)S(1)}, u32[]{:S(2)}, u32[]{:S(2)}) collective-permute-start(f32[32,768]{1,0:T(8,128)S(1)} %collective-permute-done.64.refs_4_), channel_id=1, source_target_pairs={{0,2},{1,3},{2,0},{3,1},{4,6},{5,7},{6,4},{7,5},{8,10},{9,11},{10,... | collective-permute-start | bytes 294920 | tf_op jit(solution)/shard_map/ppermute | solution.py:219
  130.7 7.9 %collective-permute-start.63 = (f32[32,768]{1,0:T(8,128)S(1)}, f32[32,768]{1,0:T(8,128)S(1)}, u32[]{:S(2)}, u32[]{:S(2)}) collective-permute-start(f32[32,768]{1,0:T(8,128)S(1)} %collective-permute-done.62.refs_8_), channel_id=1, source_target_pairs={{0,2},{1,3},{2,0},{3,1},{4,6},{5,7},{6,4},{7,5},{8,10},{9,11},{10,... | collective-permute-start | bytes 294920 | tf_op jit(solution)/shard_map/ppermute | solution.py:219
  131.7 6.9 %collective-permute-start.72 = (f32[32,768]{1,0:T(8,128)S(1)}, f32[32,768]{1,0:T(8,128)S(1)}, u32[]{:S(2)}, u32[]{:S(2)}) collective-permute-start(f32[32,768]{1,0:T(8,128)S(1)} %shard_map.79.refs_12_), channel_id=1, source_target_pairs={{0,1},{1,0},{2,3},{3,2},{4,5},{5,4},{6,7},{7,6},{8,9},{9,8},{10,11... | collective-permute-start | bytes 294920 | tf_op jit(solution)/shard_map/ppermute | solution.py:219
  148.0 6.5 %collective-permute-start.79 = (f32[32,768]{1,0:T(8,128)S(1)}, f32[32,768]{1,0:T(8,128)S(1)}, u32[]{:S(2)}, u32[]{:S(2)}) collective-permute-start(f32[32,768]{1,0:T(8,128)S(1)} %shard_map.81.refs_12_), channel_id=1, source_target_pairs={{0,12},{1,13},{2,14},{3,15},{4,0},{5,1},{6,2},{7,3},{8,4},{9,5},{1... | collective-permute-start | bytes 294920 | tf_op jit(solution)/shard_map/ppermute | solution.py:219
  149.8 7.6 %collective-permute-start.77 = (f32[32,768]{1,0:T(8,128)S(1)}, f32[32,768]{1,0:T(8,128)S(1)}, u32[]{:S(2)}, u32[]{:S(2)}) collective-permute-start(f32[32,768]{1,0:T(8,128)S(1)} %shard_map.81.refs_12_), channel_id=1, source_target_pairs={{0,4},{1,5},{2,6},{3,7},{4,8},{5,9},{6,10},{7,11},{8,12},{9,13},{1... | collective-permute-start | bytes 294920 | tf_op jit(solution)/shard_map/ppermute | solution.py:219
  150.1 8.2 %collective-permute-start.88 = (f32[32,768]{1,0:T(8,128)S(1)}, f32[32,768]{1,0:T(8,128)S(1)}, u32[]{:S(2)}, u32[]{:S(2)}) collective-permute-start(f32[32,768]{1,0:T(8,128)S(1)} %shard_map.81.refs_12_), channel_id=1, source_target_pairs={{0,2},{1,3},{2,0},{3,1},{4,6},{5,7},{6,4},{7,5},{8,10},{9,11},{10,... | collective-permute-start | bytes 294920 | tf_op jit(solution)/shard_map/ppermute | solution.py:219
  151.2 12.0 %collective-permute-start.76 = (f32[32,768]{1,0:T(8,128)S(1)}, f32[32,768]{1,0:T(8,128)S(1)}, u32[]{:S(2)}, u32[]{:S(2)}) collective-permute-start(f32[32,768]{1,0:T(8,128)S(1)} %shard_map.81.refs_12_), channel_id=1, source_target_pairs={{0,10},{1,11},{2,8},{3,9},{4,14},{5,15},{6,12},{7,13},{8,2},{9,3},... | collective-permute-start | bytes 294920 | tf_op jit(solution)/shard_map/ppermute | solution.py:219
  151.9 12.8 %collective-permute-start.75 = (f32[32,768]{1,0:T(8,128)S(1)}, f32[32,768]{1,0:T(8,128)S(1)}, u32[]{:S(2)}, u32[]{:S(2)}) collective-permute-start(f32[32,768]{1,0:T(8,128)S(1)} %shard_map.81.refs_12_), channel_id=1, source_target_pairs={{0,8},{1,9},{2,10},{3,11},{4,12},{5,13},{6,14},{7,15},{8,0},{9,1},... | collective-permute-start | bytes 294920 | tf_op jit(solution)/shard_map/ppermute | solution.py:219
  154.5 10.2 %collective-permute-start.80 = (f32[32,768]{1,0:T(8,128)S(1)}, f32[32,768]{1,0:T(8,128)S(1)}, u32[]{:S(2)}, u32[]{:S(2)}) collective-permute-start(f32[32,768]{1,0:T(8,128)S(1)} %collective-permute-done.79.refs_4_), channel_id=1, source_target_pairs={{0,2},{1,3},{2,0},{3,1},{4,6},{5,7},{6,4},{7,5},{8,10},{9,11},{10,... | collective-permute-start | bytes 294920 | tf_op jit(solution)/shard_map/ppermute | solution.py:219
  157.3 7.9 %collective-permute-start.78 = (f32[32,768]{1,0:T(8,128)S(1)}, f32[32,768]{1,0:T(8,128)S(1)}, u32[]{:S(2)}, u32[]{:S(2)}) collective-permute-start(f32[32,768]{1,0:T(8,128)S(1)} %collective-permute-done.77.refs_8_), channel_id=1, source_target_pairs={{0,2},{1,3},{2,0},{3,1},{4,6},{5,7},{6,4},{7,5},{8,10},{9,11},{10,... | collective-permute-start | bytes 294920 | tf_op jit(solution)/shard_map/ppermute | solution.py:219
  158.4 6.9 %collective-permute-start.87 = (f32[32,768]{1,0:T(8,128)S(1)}, f32[32,768]{1,0:T(8,128)S(1)}, u32[]{:S(2)}, u32[]{:S(2)}) collective-permute-start(f32[32,768]{1,0:T(8,128)S(1)} %shard_map.81.refs_12_), channel_id=1, source_target_pairs={{0,1},{1,0},{2,3},{3,2},{4,5},{5,4},{6,7},{7,6},{8,9},{9,8},{10,11... | collective-permute-start | bytes 294920 | tf_op jit(solution)/shard_map/ppermute | solution.py:219
  175.6 7.4 %collective-permute-start.96 = (f32[2,16]{1,0:T(2,128)S(1)}, f32[2,16]{1,0:T(2,128)S(1)}, u32[]{:S(2)}, u32[]{:S(2)}) collective-permute-start(f32[2,16]{1,0:T(2,128)S(1)} %get-tuple-element.41), channel_id=1, source_target_pairs={{0,14},{1,15},{2,12},{3,13},{4,2},{5,3},{6,0},{7,1},{8,6},{9,7},{1... | collective-permute-start | bytes 392 | tf_op jit(solution)/shard_map/ppermute | solution.py:219
  178.5 7.0 %collective-permute-start.94 = (f32[2,16]{1,0:T(2,128)S(1)}, f32[2,16]{1,0:T(2,128)S(1)}, u32[]{:S(2)}, u32[]{:S(2)}) collective-permute-start(f32[2,16]{1,0:T(2,128)S(1)} %get-tuple-element.41), channel_id=1, source_target_pairs={{0,10},{1,11},{2,8},{3,9},{4,14},{5,15},{6,12},{7,13},{8,2},{9,3},... | collective-permute-start | bytes 392 | tf_op jit(solution)/shard_map/ppermute | solution.py:219
  178.7 6.8 %collective-permute-start.93 = (f32[2,16]{1,0:T(2,128)S(1)}, f32[2,16]{1,0:T(2,128)S(1)}, u32[]{:S(2)}, u32[]{:S(2)}) collective-permute-start(f32[2,16]{1,0:T(2,128)S(1)} %get-tuple-element.41), channel_id=1, source_target_pairs={{0,2},{1,3},{2,0},{3,1},{4,6},{5,7},{6,4},{7,5},{8,10},{9,11},{10,... | collective-permute-start | bytes 392 | tf_op jit(solution)/shard_map/ppermute | solution.py:219
  (54 other events, 152.0 us)

commit v2 on v0

--- a/solution.py
+++ b/solution.py
@@ -238,12 +238,14 @@
         blocks[4 * far + 2] = move(own, [(i, j ^ 2) for i, j in z_pairs[far]])
         for d in order[:-1]:
             blocks[4 * d + 2] = move(blocks[4 * d], y_pairs)
-        passed = [blocks[4 * d + 2] for d in order[:-1]]
+        for d in [0] + order[:-1]:
+            blocks[4 * d + 1] = move(blocks[4 * d], c_pairs)
+            blocks[4 * d + 3] = move(blocks[4 * d + 2], c_pairs)
+        passed = [blocks[4 * d + 2] for d in order[:-1]] + [blocks[1], blocks[3]]
         pair = after(blocks[4 * far], blocks[4 * far + 2], *passed)
         blocks[4 * far], blocks[4 * far + 2] = pair
-        for d in [0] + order:
-            blocks[4 * d + 1] = move(blocks[4 * d], c_pairs)
-            blocks[4 * d + 3] = move(blocks[4 * d + 2], c_pairs)
+        blocks[4 * far + 1] = move(blocks[4 * far], c_pairs)
+        blocks[4 * far + 3] = move(blocks[4 * far + 2], c_pairs)
         args = (neighbours, *[blocks[j] for j in places], field, cross_a, cross_b, inverse)
         if step == ITERS - 1:
             sources, part = sweep(True, *args, panel_weight)

time: 188 us -> 192 us (1.021)
  waiting for transfers between devices: 60.6 us -> 69.3 us
  starting transfers between devices: 67.5 us -> 62.8 us
    ppermute x95, waiting for transfers between devices: 60.6 us -> 69.3 us  [move(): return lax.ppermute(x, 'body', pairs)]
    ppermute x95, starting transfers between devices: 67.5 us -> 62.8 us  [move(): return lax.ppermute(x, 'body', pairs)]
  transfers between devices with their start and end apart: 95 -> 95, of which waited for: 46 -> 51; matrix products, arithmetic and copies ran while one was open for 0% -> 0% of each run, Pallas kernels for 4% -> 4%
where the time goes in v2:
time: 192 us
  waiting for transfers between devices  69.3 us (36%)
  starting transfers between devices  62.8 us (33%)
  Pallas kernels  57.6 us (30%)
    ppermute x95, waiting for transfers between devices, move(): return lax.ppermute(x, 'body', pairs)  69.3 us
    ppermute x95, starting transfers between devices, move(): return lax.ppermute(x, 'body', pairs)  62.8 us
    pallas_call x6, Pallas kernels, sweep(): pl.pallas_call(functools.partial(sweep_kernel, heads, slots, places, last...  45.4 us
    pallas_call x1, Pallas kernels, body(): pl.pallas_call(near_kernel, in_specs=[HBM, VMEM], out_specs=[VMEM, VMEM],...  4.15 us
    pallas_call x1, Pallas kernels, body(): cross_b = split_late(all_blocks, same)  4.14 us
    pallas_call x1, Pallas kernels, body(): pl.pallas_call(functools.partial(first_kernel, heads), in_specs=[HBM, VME...  3.85 us
  transfers between devices with their start and end apart: 95, of which 51 were waited for; matrix products, arithmetic and copies ran while one was open for 0% of the time, Pallas kernels for 4%

profile of v2, /device:TPU:0, one launch (start us, length us, event | category | flops | bytes accessed | tf_op | source)
XLA Modules:
  0.0 192.1 jit_solution(2725185947811909029)
XLA Ops:
  1.5 3.9 %shard_map.68 = (bf16[3072,768]{1,0:T(8,128)(2,1)S(1)}, f32[32,768]{1,0:T(8,128)S(1)}) custom-call(f32[2,768,768]{2,1,0:T(8,128)} %bitcast.15, f32[32,768]{1,0:T(8,128)S(1)} %bitcast.6), custom_call_target="tpu_custom_call" | custom-call | tf_op jit(solution)/shard_map/pallas_call | solution.py:163
  5.4 3.0 %collective-permute-start.7 = (f32[32,768]{1,0:T(8,128)S(1)}, f32[32,768]{1,0:T(8,128)S(1)}, u32[]{:S(2)}, u32[]{:S(2)}) collective-permute-start(f32[32,768]{1,0:T(8,128)S(1)} %get-tuple-element.22.field_ref.refs_12_), channel_id=1, source_target_pairs={{0,2},{1,3},{2,0},{3,1},{4,6},{5,7},{6,4},{7,5},{8,10},{9,11},{10,... | collective-permute-start | bytes 294920 | tf_op jit(solution)/shard_map/ppermute | solution.py:219
  8.4 3.6 %collective-permute-start.3 = (f32[32,768]{1,0:T(8,128)S(1)}, f32[32,768]{1,0:T(8,128)S(1)}, u32[]{:S(2)}, u32[]{:S(2)}) collective-permute-start(f32[32,768]{1,0:T(8,128)S(1)} %get-tuple-element.22.field_ref.refs_12_), channel_id=1, source_target_pairs={{0,12},{1,13},{2,14},{3,15},{4,0},{5,1},{6,2},{7,3},{8,4},{9,5},{1... | collective-permute-start | bytes 294920 | tf_op jit(solution)/shard_map/ppermute | solution.py:219
  12.0 4.1 %shard_map.69 = (bf16[3072,1536]{1,0:T(8,128)(2,1)S(1)}, f32[32,768]{1,0:T(8,128)S(1)}) custom-call(f32[8,768,768]{2,1,0:T(8,128)} %bitcast.13, f32[32,768]{1,0:T(8,128)S(1)} %get-tuple-element.22.field_ref.refs_12_), custom_call_target="tpu_custom_call" | custom-call | flops 37748736 | bytes 9437184 | tf_op jit(solution)/shard_map/pallas_call | solution.py:185
  17.2 4.1 %shard_map.70.refs_2_.refs_18_ = bf16[3072,1536]{1,0:T(8,128)(2,1)S(1)} custom-call(f32[8,768,768]{2,1,0:T(8,128)} %bitcast.14, f32[32,768]{1,0:T(8,128)S(1)} %get-tuple-element.23.waited), custom_call_target="tpu_custom_call" | custom-call | flops 37748736 | bytes 9437184 | tf_op jit(solution)/shard_map/pallas_call | solution.py:235
  21.4 2.0 %collective-permute-start = (f32[32,768]{1,0:T(8,128)S(1)}, f32[32,768]{1,0:T(8,128)S(1)}, u32[]{:S(2)}, u32[]{:S(2)}) collective-permute-start(f32[32,768]{1,0:T(8,128)S(1)} %get-tuple-element.23.waited), channel_id=1, source_target_pairs={{0,8},{1,9},{2,10},{3,11},{4,12},{5,13},{6,14},{7,15},{8,0},{9,1},... | collective-permute-start | bytes 294920 | tf_op jit(solution)/shard_map/ppermute | solution.py:219
  23.4 1.5 collective-permute-start.4
  25.6 1.3 collective-permute-done.refs_0_
  28.0 2.1 %collective-permute-done.5.refs_3_.refs_6_ = f32[32,768]{1,0:T(8,128)S(1)} collective-permute-done((f32[32,768]{1,0:T(8,128)S(1)}, f32[32,768]{1,0:T(8,128)S(1)}, u32[]{:S(2)}, u32[]{:S(2)}) %collective-permute-start.5) | collective-permute-done | bytes 98336 | tf_op jit(solution)/shard_map/ppermute | solution.py:219
  32.1 7.3 %shard_map.73.refs_12_ = f32[32,768]{1,0:T(8,128)S(1)} custom-call(s32[1,4]{1,0:T(1,128)S(1)} %copy-done.2, f32[32,768]{1,0:T(8,128)S(1)} %get-tuple-element.26.refs_0_, f32[32,768]{1,0:T(8,128)S(1)} %collective-permute-done.9.refs_1_, f32[32,768]{1,0:T(8,128)S(1)} %get-tuple-element.27.refs_2_, f32[32,768]{1,0:T(8,128)S(1)} %collective-permute-done.10.refs_3_, ...), custom_call_target="tpu_custom_call" | custom-call | tf_op jit(solution)/shard_map/pallas_call | solution.py:205
  39.4 1.6 collective-permute-start.22
  41.1 3.8 %collective-permute-start.19 = (f32[32,768]{1,0:T(8,128)S(1)}, f32[32,768]{1,0:T(8,128)S(1)}, u32[]{:S(2)}, u32[]{:S(2)}) collective-permute-start(f32[32,768]{1,0:T(8,128)S(1)} %shard_map.73.refs_12_), channel_id=1, source_target_pairs={{0,12},{1,13},{2,14},{3,15},{4,0},{5,1},{6,2},{7,3},{8,4},{9,5},{1... | collective-permute-start | bytes 294920 | tf_op jit(solution)/shard_map/ppermute | solution.py:219
  45.4 2.4 %collective-permute-start.15 = (f32[32,768]{1,0:T(8,128)S(1)}, f32[32,768]{1,0:T(8,128)S(1)}, u32[]{:S(2)}, u32[]{:S(2)}) collective-permute-start(f32[32,768]{1,0:T(8,128)S(1)} %shard_map.73.refs_12_), channel_id=1, source_target_pairs={{0,8},{1,9},{2,10},{3,11},{4,12},{5,13},{6,14},{7,15},{8,0},{9,1},... | collective-permute-start | bytes 294920 | tf_op jit(solution)/shard_map/ppermute | solution.py:219
  48.1 1.3 collective-permute-start.20
  49.4 3.1 %collective-permute-done.17.refs_8_ = f32[32,768]{1,0:T(8,128)S(1)} collective-permute-done((f32[32,768]{1,0:T(8,128)S(1)}, f32[32,768]{1,0:T(8,128)S(1)}, u32[]{:S(2)}, u32[]{:S(2)}) %collective-permute-start.17) | collective-permute-done | bytes 98336 | tf_op jit(solution)/shard_map/ppermute | solution.py:219
  53.0 5.0 %collective-permute-done.16.refs_1_ = f32[32,768]{1,0:T(8,128)S(1)} collective-permute-done((f32[32,768]{1,0:T(8,128)S(1)}, f32[32,768]{1,0:T(8,128)S(1)}, u32[]{:S(2)}, u32[]{:S(2)}) %collective-permute-start.16) | collective-permute-done | bytes 98336 | tf_op jit(solution)/shard_map/ppermute | solution.py:219
  61.5 7.5 %shard_map.75.refs_12_ = f32[32,768]{1,0:T(8,128)S(1)} custom-call(s32[1,4]{1,0:T(1,128)S(1)} %copy-done.2, f32[32,768]{1,0:T(8,128)S(1)} %get-tuple-element.30.refs_0_, f32[32,768]{1,0:T(8,128)S(1)} %collective-permute-done.24.refs_1_, f32[32,768]{1,0:T(8,128)S(1)} %get-tuple-element.31.refs_2_, f32[32,768]{1,0:T(8,128)S(1)} %collective-permute-done.25.refs_3_, ...), custom_call_target="tpu_custom_call" | custom-call | tf_op jit(solution)/shard_map/pallas_call | solution.py:205
  69.0 1.5 collective-permute-start.37
  70.6 1.5 collective-permute-start.34
  73.9 1.6 collective-permute-start.30
  75.8 1.3 collective-permute-start.35
  77.1 2.5 %collective-permute-done.32.refs_8_ = f32[32,768]{1,0:T(8,128)S(1)} collective-permute-done((f32[32,768]{1,0:T(8,128)S(1)}, f32[32,768]{1,0:T(8,128)S(1)}, u32[]{:S(2)}, u32[]{:S(2)}) %collective-permute-start.32) | collective-permute-done | bytes 98336 | tf_op jit(solution)/shard_map/ppermute | solution.py:219
  80.2 5.1 %collective-permute-done.31.refs_1_ = f32[32,768]{1,0:T(8,128)S(1)} collective-permute-done((f32[32,768]{1,0:T(8,128)S(1)}, f32[32,768]{1,0:T(8,128)S(1)}, u32[]{:S(2)}, u32[]{:S(2)}) %collective-permute-start.31) | collective-permute-done | bytes 98336 | tf_op jit(solution)/shard_map/ppermute | solution.py:219
  89.0 7.4 %shard_map.77.refs_12_ = f32[32,768]{1,0:T(8,128)S(1)} custom-call(s32[1,4]{1,0:T(1,128)S(1)} %copy-done.2, f32[32,768]{1,0:T(8,128)S(1)} %get-tuple-element.32.refs_0_, f32[32,768]{1,0:T(8,128)S(1)} %collective-permute-done.39.refs_1_, f32[32,768]{1,0:T(8,128)S(1)} %get-tuple-element.33.refs_2_, f32[32,768]{1,0:T(8,128)S(1)} %collective-permute-done.40.refs_3_, ...), custom_call_target="tpu_custom_call" | custom-call | tf_op jit(solution)/shard_map/pallas_call | solution.py:205
  96.3 1.4 collective-permute-start.52
  97.7 1.3 collective-permute-start.49
  101.2 1.7 collective-permute-start.45
  102.9 1.3 collective-permute-start.50
  104.2 2.4 %collective-permute-done.47.refs_8_ = f32[32,768]{1,0:T(8,128)S(1)} collective-permute-done((f32[32,768]{1,0:T(8,128)S(1)}, f32[32,768]{1,0:T(8,128)S(1)}, u32[]{:S(2)}, u32[]{:S(2)}) %collective-permute-start.47) | collective-permute-done | bytes 98336 | tf_op jit(solution)/shard_map/ppermute | solution.py:219
  106.6 1.5 collective-permute-start.48
  108.1 5.0 %collective-permute-done.46.refs_1_ = f32[32,768]{1,0:T(8,128)S(1)} collective-permute-done((f32[32,768]{1,0:T(8,128)S(1)}, f32[32,768]{1,0:T(8,128)S(1)}, u32[]{:S(2)}, u32[]{:S(2)}) %collective-permute-start.46) | collective-permute-done | bytes 98336 | tf_op jit(solution)/shard_map/ppermute | solution.py:219
  116.7 7.6 %shard_map.79.refs_12_ = f32[32,768]{1,0:T(8,128)S(1)} custom-call(s32[1,4]{1,0:T(1,128)S(1)} %copy-done.2, f32[32,768]{1,0:T(8,128)S(1)} %get-tuple-element.34.refs_0_, f32[32,768]{1,0:T(8,128)S(1)} %collective-permute-done.54.refs_1_, f32[32,768]{1,0:T(8,128)S(1)} %get-tuple-element.35.refs_2_, f32[32,768]{1,0:T(8,128)S(1)} %collective-permute-done.55.refs_3_, ...), custom_call_target="tpu_custom_call" | custom-call | tf_op jit(solution)/shard_map/pallas_call | solution.py:205
  125.3 1.3 collective-permute-start.64
  129.2 1.6 collective-permute-start.60
  131.8 2.4 %collective-permute-done.62.refs_8_ = f32[32,768]{1,0:T(8,128)S(1)} collective-permute-done((f32[32,768]{1,0:T(8,128)S(1)}, f32[32,768]{1,0:T(8,128)S(1)}, u32[]{:S(2)}, u32[]{:S(2)}) %collective-permute-start.62) | collective-permute-done | bytes 98336 | tf_op jit(solution)/shard_map/ppermute | solution.py:219
  134.1 1.3 collective-permute-start.63
  135.4 5.1 %collective-permute-done.61.refs_1_ = f32[32,768]{1,0:T(8,128)S(1)} collective-permute-done((f32[32,768]{1,0:T(8,128)S(1)}, f32[32,768]{1,0:T(8,128)S(1)}, u32[]{:S(2)}, u32[]{:S(2)}) %collective-permute-start.61) | collective-permute-done | bytes 98336 | tf_op jit(solution)/shard_map/ppermute | solution.py:219
  144.2 7.3 %shard_map.81.refs_12_ = f32[32,768]{1,0:T(8,128)S(1)} custom-call(s32[1,4]{1,0:T(1,128)S(1)} %copy-done.2, f32[32,768]{1,0:T(8,128)S(1)} %get-tuple-element.36.refs_0_, f32[32,768]{1,0:T(8,128)S(1)} %collective-permute-done.69.refs_1_, f32[32,768]{1,0:T(8,128)S(1)} %get-tuple-element.37.refs_2_, f32[32,768]{1,0:T(8,128)S(1)} %collective-permute-done.70.refs_3_, ...), custom_call_target="tpu_custom_call" | custom-call | tf_op jit(solution)/shard_map/pallas_call | solution.py:205
  152.6 1.7 collective-permute-start.79
  156.5 1.6 collective-permute-start.75
  159.1 2.7 %collective-permute-done.77.refs_8_ = f32[32,768]{1,0:T(8,128)S(1)} collective-permute-done((f32[32,768]{1,0:T(8,128)S(1)}, f32[32,768]{1,0:T(8,128)S(1)}, u32[]{:S(2)}, u32[]{:S(2)}) %collective-permute-start.77) | collective-permute-done | bytes 98336 | tf_op jit(solution)/shard_map/ppermute | solution.py:219
  162.8 5.1 %collective-permute-done.76.refs_1_ = f32[32,768]{1,0:T(8,128)S(1)} collective-permute-done((f32[32,768]{1,0:T(8,128)S(1)}, f32[32,768]{1,0:T(8,128)S(1)}, u32[]{:S(2)}, u32[]{:S(2)}) %collective-permute-start.76) | collective-permute-done | bytes 98336 | tf_op jit(solution)/shard_map/ppermute | solution.py:219
  167.8 1.3 collective-permute-done.75.refs_0_
  171.5 8.3 %shard_map.83 = (f32[32,768]{1,0:T(8,128)}, f32[2,16]{1,0:T(2,128)S(1)}) custom-call(s32[1,4]{1,0:T(1,128)S(1)} %copy-done.2, f32[32,768]{1,0:T(8,128)S(1)} %get-tuple-element.38.refs_0_, f32[32,768]{1,0:T(8,128)S(1)} %collective-permute-done.84.refs_1_, f32[32,768]{1,0:T(8,128)S(1)} %get-tuple-element.39.refs_2_, ...), custom_call_target="tpu_custom_call" | custom-call | tf_op jit(solution)/shard_map/pallas_call | solution.py:205
  179.8 1.6 collective-permute-start.92
  182.0 1.4 collective-permute-done.92
  183.4 3.4 %collective-permute-done.91 = f32[2,16]{1,0:T(2,128)S(1)} collective-permute-done((f32[2,16]{1,0:T(2,128)S(1)}, f32[2,16]{1,0:T(2,128)S(1)}, u32[]{:S(2)}, u32[]{:S(2)}) %collective-permute-start.91) | collective-permute-done | bytes 160 | tf_op jit(solution)/shard_map/ppermute | solution.py:219
  187.9 2.5 %collective-permute-done.93 = f32[2,16]{1,0:T(2,128)S(1)} collective-permute-done((f32[2,16]{1,0:T(2,128)S(1)}, f32[2,16]{1,0:T(2,128)S(1)}, u32[]{:S(2)}, u32[]{:S(2)}) %collective-permute-start.93) | collective-permute-done | bytes 160 | tf_op jit(solution)/shard_map/ppermute | solution.py:219
  (169 shorter events, 42.0 us)
Async XLA Ops:
  5.4 19.5 %collective-permute-start.7 = (f32[32,768]{1,0:T(8,128)S(1)}, f32[32,768]{1,0:T(8,128)S(1)}, u32[]{:S(2)}, u32[]{:S(2)}) collective-permute-start(f32[32,768]{1,0:T(8,128)S(1)} %get-tuple-element.22.field_ref.refs_12_), channel_id=1, source_target_pairs={{0,2},{1,3},{2,0},{3,1},{4,6},{5,7},{6,4},{7,5},{8,10},{9,11},{10,... | collective-permute-start | bytes 294920 | tf_op jit(solution)/shard_map/ppermute | solution.py:219
  8.4 16.5 %collective-permute-start.6 = (f32[32,768]{1,0:T(8,128)S(1)}, f32[32,768]{1,0:T(8,128)S(1)}, u32[]{:S(2)}, u32[]{:S(2)}) collective-permute-start(f32[32,768]{1,0:T(8,128)S(1)} %get-tuple-element.22.field_ref.refs_12_), channel_id=1, source_target_pairs={{0,1},{1,0},{2,3},{3,2},{4,5},{5,4},{6,7},{7,6},{8,9},{9,8},{10,11... | collective-permute-start | bytes 294920 | tf_op jit(solution)/shard_map/ppermute | solution.py:219
  8.4 13.0 %collective-permute-start.3 = (f32[32,768]{1,0:T(8,128)S(1)}, f32[32,768]{1,0:T(8,128)S(1)}, u32[]{:S(2)}, u32[]{:S(2)}) collective-permute-start(f32[32,768]{1,0:T(8,128)S(1)} %get-tuple-element.22.field_ref.refs_12_), channel_id=1, source_target_pairs={{0,12},{1,13},{2,14},{3,15},{4,0},{5,1},{6,2},{7,3},{8,4},{9,5},{1... | collective-permute-start | bytes 294920 | tf_op jit(solution)/shard_map/ppermute | solution.py:219
  12.0 11.3 %collective-permute-start.2 = (f32[32,768]{1,0:T(8,128)S(1)}, f32[32,768]{1,0:T(8,128)S(1)}, u32[]{:S(2)}, u32[]{:S(2)}) collective-permute-start(f32[32,768]{1,0:T(8,128)S(1)} %get-tuple-element.22.field_ref.refs_12_), channel_id=1, source_target_pairs={{0,4},{1,5},{2,6},{3,7},{4,8},{5,9},{6,10},{7,11},{8,12},{9,13},{1... | collective-permute-start | bytes 294920 | tf_op jit(solution)/shard_map/ppermute | solution.py:219
  16.2 9.3 %collective-permute-start.1 = (f32[32,768]{1,0:T(8,128)S(1)}, f32[32,768]{1,0:T(8,128)S(1)}, u32[]{:S(2)}, u32[]{:S(2)}) collective-permute-start(f32[32,768]{1,0:T(8,128)S(1)} %get-tuple-element.23.waited), channel_id=1, source_target_pairs={{0,10},{1,11},{2,8},{3,9},{4,14},{5,15},{6,12},{7,13},{8,2},{9,3},... | collective-permute-start | bytes 294920 | tf_op jit(solution)/shard_map/ppermute | solution.py:219
  21.4 5.6 %collective-permute-start = (f32[32,768]{1,0:T(8,128)S(1)}, f32[32,768]{1,0:T(8,128)S(1)}, u32[]{:S(2)}, u32[]{:S(2)}) collective-permute-start(f32[32,768]{1,0:T(8,128)S(1)} %get-tuple-element.23.waited), channel_id=1, source_target_pairs={{0,8},{1,9},{2,10},{3,11},{4,12},{5,13},{6,14},{7,15},{8,0},{9,1},... | collective-permute-start | bytes 294920 | tf_op jit(solution)/shard_map/ppermute | solution.py:219
  24.9 5.2 %collective-permute-start.5 = (f32[32,768]{1,0:T(8,128)S(1)}, f32[32,768]{1,0:T(8,128)S(1)}, u32[]{:S(2)}, u32[]{:S(2)}) collective-permute-start(f32[32,768]{1,0:T(8,128)S(1)} %get-tuple-element.25.refs_4_), channel_id=1, source_target_pairs={{0,2},{1,3},{2,0},{3,1},{4,6},{5,7},{6,4},{7,5},{8,10},{9,11},{10,... | collective-permute-start | bytes 294920 | tf_op jit(solution)/shard_map/ppermute | solution.py:219
  39.4 6.0 %collective-permute-start.22 = (f32[32,768]{1,0:T(8,128)S(1)}, f32[32,768]{1,0:T(8,128)S(1)}, u32[]{:S(2)}, u32[]{:S(2)}) collective-permute-start(f32[32,768]{1,0:T(8,128)S(1)} %shard_map.73.refs_12_), channel_id=1, source_target_pairs={{0,2},{1,3},{2,0},{3,1},{4,6},{5,7},{6,4},{7,5},{8,10},{9,11},{10,... | collective-permute-start | bytes 294920 | tf_op jit(solution)/shard_map/ppermute | solution.py:219
  41.0 6.8 %collective-permute-start.21 = (f32[32,768]{1,0:T(8,128)S(1)}, f32[32,768]{1,0:T(8,128)S(1)}, u32[]{:S(2)}, u32[]{:S(2)}) collective-permute-start(f32[32,768]{1,0:T(8,128)S(1)} %shard_map.73.refs_12_), channel_id=1, source_target_pairs={{0,1},{1,0},{2,3},{3,2},{4,5},{5,4},{6,7},{7,6},{8,9},{9,8},{10,11... | collective-permute-start | bytes 294920 | tf_op jit(solution)/shard_map/ppermute | solution.py:219
  41.1 7.0 %collective-permute-start.19 = (f32[32,768]{1,0:T(8,128)S(1)}, f32[32,768]{1,0:T(8,128)S(1)}, u32[]{:S(2)}, u32[]{:S(2)}) collective-permute-start(f32[32,768]{1,0:T(8,128)S(1)} %shard_map.73.refs_12_), channel_id=1, source_target_pairs={{0,12},{1,13},{2,14},{3,15},{4,0},{5,1},{6,2},{7,3},{8,4},{9,5},{1... | collective-permute-start | bytes 294920 | tf_op jit(solution)/shard_map/ppermute | solution.py:219
  44.9 7.5 %collective-permute-start.17 = (f32[32,768]{1,0:T(8,128)S(1)}, f32[32,768]{1,0:T(8,128)S(1)}, u32[]{:S(2)}, u32[]{:S(2)}) collective-permute-start(f32[32,768]{1,0:T(8,128)S(1)} %shard_map.73.refs_12_), channel_id=1, source_target_pairs={{0,4},{1,5},{2,6},{3,7},{4,8},{5,9},{6,10},{7,11},{8,12},{9,13},{1... | collective-permute-start | bytes 294920 | tf_op jit(solution)/shard_map/ppermute | solution.py:219
  44.9 13.0 %collective-permute-start.16 = (f32[32,768]{1,0:T(8,128)S(1)}, f32[32,768]{1,0:T(8,128)S(1)}, u32[]{:S(2)}, u32[]{:S(2)}) collective-permute-start(f32[32,768]{1,0:T(8,128)S(1)} %shard_map.73.refs_12_), channel_id=1, source_target_pairs={{0,10},{1,11},{2,8},{3,9},{4,14},{5,15},{6,12},{7,13},{8,2},{9,3},... | collective-permute-start | bytes 294920 | tf_op jit(solution)/shard_map/ppermute | solution.py:219
  45.4 13.6 %collective-permute-start.15 = (f32[32,768]{1,0:T(8,128)S(1)}, f32[32,768]{1,0:T(8,128)S(1)}, u32[]{:S(2)}, u32[]{:S(2)}) collective-permute-start(f32[32,768]{1,0:T(8,128)S(1)} %shard_map.73.refs_12_), channel_id=1, source_target_pairs={{0,8},{1,9},{2,10},{3,11},{4,12},{5,13},{6,14},{7,15},{8,0},{9,1},... | collective-permute-start | bytes 294920 | tf_op jit(solution)/shard_map/ppermute | solution.py:219
  47.8 11.3 %collective-permute-start.23 = (f32[32,768]{1,0:T(8,128)S(1)}, f32[32,768]{1,0:T(8,128)S(1)}, u32[]{:S(2)}, u32[]{:S(2)}) collective-permute-start(f32[32,768]{1,0:T(8,128)S(1)} %collective-permute-done.22.refs_14_), channel_id=1, source_target_pairs={{0,1},{1,0},{2,3},{3,2},{4,5},{5,4},{6,7},{7,6},{8,9},{9,8},{10,11... | collective-permute-start | bytes 294920 | tf_op jit(solution)/shard_map/ppermute | solution.py:219
  48.1 11.0 %collective-permute-start.20 = (f32[32,768]{1,0:T(8,128)S(1)}, f32[32,768]{1,0:T(8,128)S(1)}, u32[]{:S(2)}, u32[]{:S(2)}) collective-permute-start(f32[32,768]{1,0:T(8,128)S(1)} %collective-permute-done.19.refs_4_), channel_id=1, source_target_pairs={{0,2},{1,3},{2,0},{3,1},{4,6},{5,7},{6,4},{7,5},{8,10},{9,11},{10,... | collective-permute-start | bytes 294920 | tf_op jit(solution)/shard_map/ppermute | solution.py:219
  52.5 6.6 %collective-permute-start.18 = (f32[32,768]{1,0:T(8,128)S(1)}, f32[32,768]{1,0:T(8,128)S(1)}, u32[]{:S(2)}, u32[]{:S(2)}) collective-permute-start(f32[32,768]{1,0:T(8,128)S(1)} %collective-permute-done.17.refs_8_), channel_id=1, source_target_pairs={{0,2},{1,3},{2,0},{3,1},{4,6},{5,7},{6,4},{7,5},{8,10},{9,11},{10,... | collective-permute-start | bytes 294920 | tf_op jit(solution)/shard_map/ppermute | solution.py:219
  70.6 5.2 %collective-permute-start.34 = (f32[32,768]{1,0:T(8,128)S(1)}, f32[32,768]{1,0:T(8,128)S(1)}, u32[]{:S(2)}, u32[]{:S(2)}) collective-permute-start(f32[32,768]{1,0:T(8,128)S(1)} %shard_map.75.refs_12_), channel_id=1, source_target_pairs={{0,12},{1,13},{2,14},{3,15},{4,0},{5,1},{6,2},{7,3},{8,4},{9,5},{1... | collective-permute-start | bytes 294920 | tf_op jit(solution)/shard_map/ppermute | solution.py:219
  72.0 7.5 %collective-permute-start.32 = (f32[32,768]{1,0:T(8,128)S(1)}, f32[32,768]{1,0:T(8,128)S(1)}, u32[]{:S(2)}, u32[]{:S(2)}) collective-permute-start(f32[32,768]{1,0:T(8,128)S(1)} %shard_map.75.refs_12_), channel_id=1, source_target_pairs={{0,4},{1,5},{2,6},{3,7},{4,8},{5,9},{6,10},{7,11},{8,12},{9,13},{1... | collective-permute-start | bytes 294920 | tf_op jit(solution)/shard_map/ppermute | solution.py:219
  72.6 12.7 %collective-permute-start.31 = (f32[32,768]{1,0:T(8,128)S(1)}, f32[32,768]{1,0:T(8,128)S(1)}, u32[]{:S(2)}, u32[]{:S(2)}) collective-permute-start(f32[32,768]{1,0:T(8,128)S(1)} %shard_map.75.refs_12_), channel_id=1, source_target_pairs={{0,10},{1,11},{2,8},{3,9},{4,14},{5,15},{6,12},{7,13},{8,2},{9,3},... | collective-permute-start | bytes 294920 | tf_op jit(solution)/shard_map/ppermute | solution.py:219
  73.9 12.6 %collective-permute-start.30 = (f32[32,768]{1,0:T(8,128)S(1)}, f32[32,768]{1,0:T(8,128)S(1)}, u32[]{:S(2)}, u32[]{:S(2)}) collective-permute-start(f32[32,768]{1,0:T(8,128)S(1)} %shard_map.75.refs_12_), channel_id=1, source_target_pairs={{0,8},{1,9},{2,10},{3,11},{4,12},{5,13},{6,14},{7,15},{8,0},{9,1},... | collective-permute-start | bytes 294920 | tf_op jit(solution)/shard_map/ppermute | solution.py:219
  75.5 11.0 %collective-permute-start.38 = (f32[32,768]{1,0:T(8,128)S(1)}, f32[32,768]{1,0:T(8,128)S(1)}, u32[]{:S(2)}, u32[]{:S(2)}) collective-permute-start(f32[32,768]{1,0:T(8,128)S(1)} %collective-permute-done.37.refs_14_), channel_id=1, source_target_pairs={{0,1},{1,0},{2,3},{3,2},{4,5},{5,4},{6,7},{7,6},{8,9},{9,8},{10,11... | collective-permute-start | bytes 294920 | tf_op jit(solution)/shard_map/ppermute | solution.py:219
  75.8 10.8 %collective-permute-start.35 = (f32[32,768]{1,0:T(8,128)S(1)}, f32[32,768]{1,0:T(8,128)S(1)}, u32[]{:S(2)}, u32[]{:S(2)}) collective-permute-start(f32[32,768]{1,0:T(8,128)S(1)} %collective-permute-done.34.refs_4_), channel_id=1, source_target_pairs={{0,2},{1,3},{2,0},{3,1},{4,6},{5,7},{6,4},{7,5},{8,10},{9,11},{10,... | collective-permute-start | bytes 294920 | tf_op jit(solution)/shard_map/ppermute | solution.py:219
  79.5 7.0 %collective-permute-start.33 = (f32[32,768]{1,0:T(8,128)S(1)}, f32[32,768]{1,0:T(8,128)S(1)}, u32[]{:S(2)}, u32[]{:S(2)}) collective-permute-start(f32[32,768]{1,0:T(8,128)S(1)} %collective-permute-done.32.refs_8_), channel_id=1, source_target_pairs={{0,2},{1,3},{2,0},{3,1},{4,6},{5,7},{6,4},{7,5},{8,10},{9,11},{10,... | collective-permute-start | bytes 294920 | tf_op jit(solution)/shard_map/ppermute | solution.py:219
  97.7 5.2 %collective-permute-start.51 = (f32[32,768]{1,0:T(8,128)S(1)}, f32[32,768]{1,0:T(8,128)S(1)}, u32[]{:S(2)}, u32[]{:S(2)}) collective-permute-start(f32[32,768]{1,0:T(8,128)S(1)} %shard_map.77.refs_12_), channel_id=1, source_target_pairs={{0,1},{1,0},{2,3},{3,2},{4,5},{5,4},{6,7},{7,6},{8,9},{9,8},{10,11... | collective-permute-start | bytes 294920 | tf_op jit(solution)/shard_map/ppermute | solution.py:219
  97.7 5.2 %collective-permute-start.49 = (f32[32,768]{1,0:T(8,128)S(1)}, f32[32,768]{1,0:T(8,128)S(1)}, u32[]{:S(2)}, u32[]{:S(2)}) collective-permute-start(f32[32,768]{1,0:T(8,128)S(1)} %shard_map.77.refs_12_), channel_id=1, source_target_pairs={{0,12},{1,13},{2,14},{3,15},{4,0},{5,1},{6,2},{7,3},{8,4},{9,5},{1... | collective-permute-start | bytes 294920 | tf_op jit(solution)/shard_map/ppermute | solution.py:219
  99.1 7.5 %collective-permute-start.47 = (f32[32,768]{1,0:T(8,128)S(1)}, f32[32,768]{1,0:T(8,128)S(1)}, u32[]{:S(2)}, u32[]{:S(2)}) collective-permute-start(f32[32,768]{1,0:T(8,128)S(1)} %shard_map.77.refs_12_), channel_id=1, source_target_pairs={{0,4},{1,5},{2,6},{3,7},{4,8},{5,9},{6,10},{7,11},{8,12},{9,13},{1... | collective-permute-start | bytes 294920 | tf_op jit(solution)/shard_map/ppermute | solution.py:219
  99.8 13.4 %collective-permute-start.46 = (f32[32,768]{1,0:T(8,128)S(1)}, f32[32,768]{1,0:T(8,128)S(1)}, u32[]{:S(2)}, u32[]{:S(2)}) collective-permute-start(f32[32,768]{1,0:T(8,128)S(1)} %shard_map.77.refs_12_), channel_id=1, source_target_pairs={{0,10},{1,11},{2,8},{3,9},{4,14},{5,15},{6,12},{7,13},{8,2},{9,3},... | collective-permute-start | bytes 294920 | tf_op jit(solution)/shard_map/ppermute | solution.py:219
  101.2 13.0 %collective-permute-start.45 = (f32[32,768]{1,0:T(8,128)S(1)}, f32[32,768]{1,0:T(8,128)S(1)}, u32[]{:S(2)}, u32[]{:S(2)}) collective-permute-start(f32[32,768]{1,0:T(8,128)S(1)} %shard_map.77.refs_12_), channel_id=1, source_target_pairs={{0,8},{1,9},{2,10},{3,11},{4,12},{5,13},{6,14},{7,15},{8,0},{9,1},... | collective-permute-start | bytes 294920 | tf_op jit(solution)/shard_map/ppermute | solution.py:219
  102.9 11.3 %collective-permute-start.53 = (f32[32,768]{1,0:T(8,128)S(1)}, f32[32,768]{1,0:T(8,128)S(1)}, u32[]{:S(2)}, u32[]{:S(2)}) collective-permute-start(f32[32,768]{1,0:T(8,128)S(1)} %collective-permute-done.52.refs_14_), channel_id=1, source_target_pairs={{0,1},{1,0},{2,3},{3,2},{4,5},{5,4},{6,7},{7,6},{8,9},{9,8},{10,11... | collective-permute-start | bytes 294920 | tf_op jit(solution)/shard_map/ppermute | solution.py:219
  102.9 11.3 %collective-permute-start.50 = (f32[32,768]{1,0:T(8,128)S(1)}, f32[32,768]{1,0:T(8,128)S(1)}, u32[]{:S(2)}, u32[]{:S(2)}) collective-permute-start(f32[32,768]{1,0:T(8,128)S(1)} %collective-permute-done.49.refs_4_), channel_id=1, source_target_pairs={{0,2},{1,3},{2,0},{3,1},{4,6},{5,7},{6,4},{7,5},{8,10},{9,11},{10,... | collective-permute-start | bytes 294920 | tf_op jit(solution)/shard_map/ppermute | solution.py:219
  106.6 7.7 %collective-permute-start.48 = (f32[32,768]{1,0:T(8,128)S(1)}, f32[32,768]{1,0:T(8,128)S(1)}, u32[]{:S(2)}, u32[]{:S(2)}) collective-permute-start(f32[32,768]{1,0:T(8,128)S(1)} %collective-permute-done.47.refs_8_), channel_id=1, source_target_pairs={{0,2},{1,3},{2,0},{3,1},{4,6},{5,7},{6,4},{7,5},{8,10},{9,11},{10,... | collective-permute-start | bytes 294920 | tf_op jit(solution)/shard_map/ppermute | solution.py:219
  125.3 5.5 %collective-permute-start.66 = (f32[32,768]{1,0:T(8,128)S(1)}, f32[32,768]{1,0:T(8,128)S(1)}, u32[]{:S(2)}, u32[]{:S(2)}) collective-permute-start(f32[32,768]{1,0:T(8,128)S(1)} %shard_map.79.refs_12_), channel_id=1, source_target_pairs={{0,1},{1,0},{2,3},{3,2},{4,5},{5,4},{6,7},{7,6},{8,9},{9,8},{10,11... | collective-permute-start | bytes 294920 | tf_op jit(solution)/shard_map/ppermute | solution.py:219
  125.3 5.5 %collective-permute-start.64 = (f32[32,768]{1,0:T(8,128)S(1)}, f32[32,768]{1,0:T(8,128)S(1)}, u32[]{:S(2)}, u32[]{:S(2)}) collective-permute-start(f32[32,768]{1,0:T(8,128)S(1)} %shard_map.79.refs_12_), channel_id=1, source_target_pairs={{0,12},{1,13},{2,14},{3,15},{4,0},{5,1},{6,2},{7,3},{8,4},{9,5},{1... | collective-permute-start | bytes 294920 | tf_op jit(solution)/shard_map/ppermute | solution.py:219
  126.6 7.5 %collective-permute-start.62 = (f32[32,768]{1,0:T(8,128)S(1)}, f32[32,768]{1,0:T(8,128)S(1)}, u32[]{:S(2)}, u32[]{:S(2)}) collective-permute-start(f32[32,768]{1,0:T(8,128)S(1)} %shard_map.79.refs_12_), channel_id=1, source_target_pairs={{0,4},{1,5},{2,6},{3,7},{4,8},{5,9},{6,10},{7,11},{8,12},{9,13},{1... | collective-permute-start | bytes 294920 | tf_op jit(solution)/shard_map/ppermute | solution.py:219
  127.3 13.3 %collective-permute-start.61 = (f32[32,768]{1,0:T(8,128)S(1)}, f32[32,768]{1,0:T(8,128)S(1)}, u32[]{:S(2)}, u32[]{:S(2)}) collective-permute-start(f32[32,768]{1,0:T(8,128)S(1)} %shard_map.79.refs_12_), channel_id=1, source_target_pairs={{0,10},{1,11},{2,8},{3,9},{4,14},{5,15},{6,12},{7,13},{8,2},{9,3},... | collective-permute-start | bytes 294920 | tf_op jit(solution)/shard_map/ppermute | solution.py:219
  129.2 12.6 %collective-permute-start.60 = (f32[32,768]{1,0:T(8,128)S(1)}, f32[32,768]{1,0:T(8,128)S(1)}, u32[]{:S(2)}, u32[]{:S(2)}) collective-permute-start(f32[32,768]{1,0:T(8,128)S(1)} %shard_map.79.refs_12_), channel_id=1, source_target_pairs={{0,8},{1,9},{2,10},{3,11},{4,12},{5,13},{6,14},{7,15},{8,0},{9,1},... | collective-permute-start | bytes 294920 | tf_op jit(solution)/shard_map/ppermute | solution.py:219
  130.7 11.0 %collective-permute-start.68 = (f32[32,768]{1,0:T(8,128)S(1)}, f32[32,768]{1,0:T(8,128)S(1)}, u32[]{:S(2)}, u32[]{:S(2)}) collective-permute-start(f32[32,768]{1,0:T(8,128)S(1)} %collective-permute-done.67.refs_14_), channel_id=1, source_target_pairs={{0,1},{1,0},{2,3},{3,2},{4,5},{5,4},{6,7},{7,6},{8,9},{9,8},{10,11... | collective-permute-start | bytes 294920 | tf_op jit(solution)/shard_map/ppermute | solution.py:219
  130.8 11.0 %collective-permute-start.65 = (f32[32,768]{1,0:T(8,128)S(1)}, f32[32,768]{1,0:T(8,128)S(1)}, u32[]{:S(2)}, u32[]{:S(2)}) collective-permute-start(f32[32,768]{1,0:T(8,128)S(1)} %collective-permute-done.64.refs_4_), channel_id=1, source_target_pairs={{0,2},{1,3},{2,0},{3,1},{4,6},{5,7},{6,4},{7,5},{8,10},{9,11},{10,... | collective-permute-start | bytes 294920 | tf_op jit(solution)/shard_map/ppermute | solution.py:219
  134.1 7.7 %collective-permute-start.63 = (f32[32,768]{1,0:T(8,128)S(1)}, f32[32,768]{1,0:T(8,128)S(1)}, u32[]{:S(2)}, u32[]{:S(2)}) collective-permute-start(f32[32,768]{1,0:T(8,128)S(1)} %collective-permute-done.62.refs_8_), channel_id=1, source_target_pairs={{0,2},{1,3},{2,0},{3,1},{4,6},{5,7},{6,4},{7,5},{8,10},{9,11},{10,... | collective-permute-start | bytes 294920 | tf_op jit(solution)/shard_map/ppermute | solution.py:219
  152.6 5.4 %collective-permute-start.81 = (f32[32,768]{1,0:T(8,128)S(1)}, f32[32,768]{1,0:T(8,128)S(1)}, u32[]{:S(2)}, u32[]{:S(2)}) collective-permute-start(f32[32,768]{1,0:T(8,128)S(1)} %shard_map.81.refs_12_), channel_id=1, source_target_pairs={{0,1},{1,0},{2,3},{3,2},{4,5},{5,4},{6,7},{7,6},{8,9},{9,8},{10,11... | collective-permute-start | bytes 294920 | tf_op jit(solution)/shard_map/ppermute | solution.py:219
  152.6 5.4 %collective-permute-start.79 = (f32[32,768]{1,0:T(8,128)S(1)}, f32[32,768]{1,0:T(8,128)S(1)}, u32[]{:S(2)}, u32[]{:S(2)}) collective-permute-start(f32[32,768]{1,0:T(8,128)S(1)} %shard_map.81.refs_12_), channel_id=1, source_target_pairs={{0,12},{1,13},{2,14},{3,15},{4,0},{5,1},{6,2},{7,3},{8,4},{9,5},{1... | collective-permute-start | bytes 294920 | tf_op jit(solution)/shard_map/ppermute | solution.py:219
  154.3 7.5 %collective-permute-start.77 = (f32[32,768]{1,0:T(8,128)S(1)}, f32[32,768]{1,0:T(8,128)S(1)}, u32[]{:S(2)}, u32[]{:S(2)}) collective-permute-start(f32[32,768]{1,0:T(8,128)S(1)} %shard_map.81.refs_12_), channel_id=1, source_target_pairs={{0,4},{1,5},{2,6},{3,7},{4,8},{5,9},{6,10},{7,11},{8,12},{9,13},{1... | collective-permute-start | bytes 294920 | tf_op jit(solution)/shard_map/ppermute | solution.py:219
  154.6 13.2 %collective-permute-start.76 = (f32[32,768]{1,0:T(8,128)S(1)}, f32[32,768]{1,0:T(8,128)S(1)}, u32[]{:S(2)}, u32[]{:S(2)}) collective-permute-start(f32[32,768]{1,0:T(8,128)S(1)} %shard_map.81.refs_12_), channel_id=1, source_target_pairs={{0,10},{1,11},{2,8},{3,9},{4,14},{5,15},{6,12},{7,13},{8,2},{9,3},... | collective-permute-start | bytes 294920 | tf_op jit(solution)/shard_map/ppermute | solution.py:219
  156.5 12.6 %collective-permute-start.75 = (f32[32,768]{1,0:T(8,128)S(1)}, f32[32,768]{1,0:T(8,128)S(1)}, u32[]{:S(2)}, u32[]{:S(2)}) collective-permute-start(f32[32,768]{1,0:T(8,128)S(1)} %shard_map.81.refs_12_), channel_id=1, source_target_pairs={{0,8},{1,9},{2,10},{3,11},{4,12},{5,13},{6,14},{7,15},{8,0},{9,1},... | collective-permute-start | bytes 294920 | tf_op jit(solution)/shard_map/ppermute | solution.py:219
  158.0 11.1 %collective-permute-start.83 = (f32[32,768]{1,0:T(8,128)S(1)}, f32[32,768]{1,0:T(8,128)S(1)}, u32[]{:S(2)}, u32[]{:S(2)}) collective-permute-start(f32[32,768]{1,0:T(8,128)S(1)} %collective-permute-done.82.refs_14_), channel_id=1, source_target_pairs={{0,1},{1,0},{2,3},{3,2},{4,5},{5,4},{6,7},{7,6},{8,9},{9,8},{10,11... | collective-permute-start | bytes 294920 | tf_op jit(solution)/shard_map/ppermute | solution.py:219
  158.0 11.1 %collective-permute-start.80 = (f32[32,768]{1,0:T(8,128)S(1)}, f32[32,768]{1,0:T(8,128)S(1)}, u32[]{:S(2)}, u32[]{:S(2)}) collective-permute-start(f32[32,768]{1,0:T(8,128)S(1)} %collective-permute-done.79.refs_4_), channel_id=1, source_target_pairs={{0,2},{1,3},{2,0},{3,1},{4,6},{5,7},{6,4},{7,5},{8,10},{9,11},{10,... | collective-permute-start | bytes 294920 | tf_op jit(solution)/shard_map/ppermute | solution.py:219
  161.8 7.3 %collective-permute-start.78 = (f32[32,768]{1,0:T(8,128)S(1)}, f32[32,768]{1,0:T(8,128)S(1)}, u32[]{:S(2)}, u32[]{:S(2)}) collective-permute-start(f32[32,768]{1,0:T(8,128)S(1)} %collective-permute-done.77.refs_8_), channel_id=1, source_target_pairs={{0,2},{1,3},{2,0},{3,1},{4,6},{5,7},{6,4},{7,5},{8,10},{9,11},{10,... | collective-permute-start | bytes 294920 | tf_op jit(solution)/shard_map/ppermute | solution.py:219
  181.4 5.4 %collective-permute-start.91 = (f32[2,16]{1,0:T(2,128)S(1)}, f32[2,16]{1,0:T(2,128)S(1)}, u32[]{:S(2)}, u32[]{:S(2)}) collective-permute-start(f32[2,16]{1,0:T(2,128)S(1)} %get-tuple-element.41), channel_id=1, source_target_pairs={{0,4},{1,5},{2,6},{3,7},{4,8},{5,9},{6,10},{7,11},{8,12},{9,13},{1... | collective-permute-start | bytes 392 | tf_op jit(solution)/shard_map/ppermute | solution.py:219
  (51 other events, 158.6 us)
